TPU v7x, 32 devices: a whole 2x2x4 slice. The times are simulated.
32 devices in a mesh: section: 2 (over x), fsdp: 16 (over z, y, core).
Axes of the slice: x: 2, y: 2, z: 4, core: 2. Of those that a mesh axis runs over, the one named last changes fastest.
Arguments:
- images: bfloat16 [4, 64, 196, 512], P(None, 'fsdp'), may hold values from -6 to 6
- live_counts: int32 [4, 16], P(None, 'fsdp'), may hold values from 1 to 4, as said below
- norm_gains: bfloat16 [2, 2, 512], P('section', None, 'fsdp'), may hold values from 0.099609375 to 1.8984375
- vectors: bfloat16 [2, 6, 512], P('section', None, 'fsdp'), may hold values from -3 to 3
- qkv_weight: bfloat16 [2, 512, 1536], P('section', 'fsdp'), may hold values from -0.25 to 0.25
- proj_weight: bfloat16 [2, 512, 512], P('section', 'fsdp'), may hold values from -0.5 to 0.5
- hidden_weight: bfloat16 [2, 512, 2048], P('section', 'fsdp'), may hold values from -0.25 to 0.25
- hidden_bias: bfloat16 [2, 2048], P('section', 'fsdp'), may hold values from -3 to 3
- out_weight: bfloat16 [2, 2048, 512], P('section', 'fsdp'), may hold values from -0.125 to 0.125
- bias_table: float32 [2, 169, 16], P('section'), may hold values from -4 to 4
- out_grad: bfloat16 [4, 64, 196, 512], P(None, 'fsdp'), may hold values from -6 to 6
Outputs:
- layer_outputs: bfloat16 [2, 4, 64, 196, 512], P('section', None, 'fsdp')
- input_grads: float32 [2, 4, 64, 196, 512], P('section', None, 'fsdp')
- grad_norm_gains: float32 [2, 2, 512], P('section', None, 'fsdp')
- grad_vectors: float32 [2, 6, 512], P('section', None, 'fsdp')
- grad_qkv: float32 [2, 512, 1536], P('section', 'fsdp')
- grad_proj: float32 [2, 512, 512], P('section', 'fsdp')
- grad_hidden_weight: float32 [2, 512, 2048], P('section', 'fsdp')
- grad_hidden_bias: float32 [2, 2048], P('section', 'fsdp')
- grad_out_weight: float32 [2, 2048, 512], P('section', 'fsdp')
- grad_bias_table: float32 [2, 169, 16], P('section')
Inputs may be any that keep to these rules, and one draw needn't show every extreme that they name: In each micro-batch the live images of an index of fsdp are the first live_counts of its 4 slots; some index has all 4 live and some has one.
All inputs are finite; a program needn't handle non-finite values.
Results may differ from a plain program's by a relative error of at most 0.019.
Values may be sent and summed in bfloat16 or wider, within the bound.
No kernel may reach another device: no remote copies, remote signals or barrier semaphores. Data moves between devices by JAX's collectives and lax.ppermute only.
A program may use at most 384 MiB of HBM per device.

v0:
```python
import math

import jax
import jax.numpy as jnp
from jax import lax
from jax.sharding import PartitionSpec as P

WIN = 7
GRID = 14
SHIFT = 3
TABLE = 169


eps = 1e-05
highest = lax.Precision.HIGHEST


def from_behind(value, axis, by):
    size = lax.axis_size(axis)
    pairs = [(i, i + by) for i in range(size) if 0 <= i + by < size]
    return lax.ppermute(value, axis, pairs)


def normalize(values):
    center = values - jnp.mean(values, axis=-1, keepdims=True)
    inverse = lax.rsqrt(jnp.mean(center * center, axis=-1, keepdims=True) + eps)
    return (center * inverse, inverse)


def norm_backward(grad_hat, norm_hat, inverse):
    return inverse * (
        grad_hat
        - jnp.mean(grad_hat, axis=-1, keepdims=True)
        - norm_hat * jnp.mean(grad_hat * norm_hat, axis=-1, keepdims=True)
    )


def gelu_slope(values):
    return (
        0.5 * (1.0 + lax.erf(values * 0.5**0.5))
        + values * jnp.exp(-0.5 * values * values) * (0.5 / math.pi) ** 0.5
    )


def inner_rows(left_rows, right_rows):
    return lax.dot_general(
        left_rows, right_rows, (((0,), (0,)), ((), ())), preferred_element_type=jnp.float32
    )


def times_back(left_rows, matrix):
    return lax.dot_general(
        left_rows, matrix, (((1,), (1,)), ((), ())), preferred_element_type=jnp.float32
    )


def to_windows(values, shifted):
    features = values.shape[-1]
    grid_cells = values.reshape(-1, GRID, GRID, features)
    grid_cells = jnp.where(shifted, jnp.roll(grid_cells, (-SHIFT, -SHIFT), (1, 2)), grid_cells)
    side_count = GRID // WIN
    window_parts = grid_cells.reshape(-1, side_count, WIN, side_count, WIN, features)
    return window_parts.transpose(0, 1, 3, 2, 4, 5).reshape(-1, WIN * WIN, features)


def from_windows(blocks, shifted):
    features = blocks.shape[-1]
    side_count = GRID // WIN
    window_parts = blocks.reshape(-1, side_count, side_count, WIN, WIN, features).transpose(
        0, 1, 3, 2, 4, 5
    )
    grid_cells = window_parts.reshape(-1, GRID, GRID, features)
    grid_cells = jnp.where(shifted, jnp.roll(grid_cells, (SHIFT, SHIFT), (1, 2)), grid_cells)
    return grid_cells.reshape(-1, GRID * GRID, features)


def offset_onehot():
    places = jnp.arange(WIN * WIN)
    row_index = places // WIN
    columns = places % WIN
    offsets = (
        (row_index[:, None] - row_index[None, :] + WIN - 1) * (2 * WIN - 1)
        + columns[:, None]
        - columns[None, :]
        + WIN
        - 1
    )
    return (offsets.reshape(-1)[:, None] == jnp.arange(TABLE)[None, :]).astype(jnp.float32)


def region_mask():
    line_index = jnp.arange(GRID)
    band_index = (line_index >= GRID - WIN).astype(jnp.int32) + (line_index >= GRID - SHIFT).astype(
        jnp.int32
    )
    region = band_index[:, None] * 3 + band_index[None, :]
    side_count = GRID // WIN
    region = (
        region.reshape(side_count, WIN, side_count, WIN)
        .transpose(0, 2, 1, 3)
        .reshape(-1, WIN * WIN)
    )
    return jnp.where(region[:, :, None] != region[:, None, :], -100.0, 0.0).astype(jnp.float32)


def layer_forward(inputs, live_mask, params, shifted, position_bias, region_bias):
    gain_rows, vector_rows, qkv_mat, proj_mat, expand_mat, expand_bias, contract_mat = params
    gain_rows = gain_rows.astype(jnp.float32)
    vector_rows = vector_rows.astype(jnp.float32)
    features = inputs.shape[-1]
    head_count = position_bias.shape[0]
    head_size = features // head_count
    field_vals = inputs.astype(jnp.float32)
    first_hat, first_inv = normalize(field_vals)
    first_norm = (first_hat * gain_rows[0] + vector_rows[0]).astype(jnp.bfloat16)
    blocks = to_windows(first_norm, shifted).reshape(-1, features)
    qkv_bias = jnp.concatenate([vector_rows[1], jnp.zeros_like(vector_rows[1]), vector_rows[2]])
    projected = (jnp.dot(blocks, qkv_mat, preferred_element_type=jnp.float32) + qkv_bias).astype(
        jnp.bfloat16
    )
    window_count = projected.shape[0] // (WIN * WIN)
    pieces = projected.reshape(window_count, WIN * WIN, 3, head_count, head_size)
    queries = pieces[:, :, 0]
    key_rows = pieces[:, :, 1]
    values_in = pieces[:, :, 2]
    scores = jnp.einsum(
        "wihc,wjhc->whij", queries, key_rows, preferred_element_type=jnp.float32
    ) * head_size ** (-0.5)
    scores = (
        scores.reshape(-1, (GRID // WIN) ** 2, head_count, WIN * WIN, WIN * WIN)
        + position_bias[None, None]
        + region_bias[None, :, None]
    )
    attn_probs = jax.nn.softmax(scores, axis=-1).reshape(
        window_count, head_count, WIN * WIN, WIN * WIN
    )
    probs_low = attn_probs.astype(jnp.bfloat16)
    mixed_out = (
        jnp.einsum("whij,wjhc->wihc", probs_low, values_in, preferred_element_type=jnp.float32)
        .astype(jnp.bfloat16)
        .reshape(-1, features)
    )
    attended = jnp.dot(mixed_out, proj_mat, preferred_element_type=jnp.float32) + vector_rows[3]
    residual = field_vals + from_windows(
        attended.reshape(window_count, WIN * WIN, features), shifted
    )
    second_hat, second_inv = normalize(residual)
    second_norm = (
        (second_hat * gain_rows[1] + vector_rows[4]).astype(jnp.bfloat16).reshape(-1, features)
    )
    hidden = jnp.dot(
        second_norm, expand_mat, preferred_element_type=jnp.float32
    ) + expand_bias.astype(jnp.float32)
    active = jax.nn.gelu(hidden, approximate=False).astype(jnp.bfloat16)
    branch = jnp.dot(active, contract_mat, preferred_element_type=jnp.float32) + vector_rows[5]
    result = (residual + branch.reshape(residual.shape)) * live_mask[:, None, None]
    saved = (
        first_hat,
        first_inv,
        blocks,
        queries,
        key_rows,
        values_in,
        attn_probs,
        probs_low,
        mixed_out,
        second_hat,
        second_inv,
        second_norm,
        hidden,
        active,
    )
    return (result, saved)


def backward_inputs(
    inputs, live_mask, params, shifted, position_bias, region_bias, cotangent, saved
):
    unused, saved = layer_forward(inputs, live_mask, params, shifted, position_bias, region_bias)
    (
        first_hat,
        first_inv,
        blocks,
        queries,
        key_rows,
        values_in,
        attn_probs,
        probs_low,
        mixed_out,
        second_hat,
        second_inv,
        second_norm,
        hidden,
        active,
    ) = saved
    gain_rows, vector_rows, qkv_mat, proj_mat, expand_mat, expand_bias, contract_mat = params
    gain_rows = gain_rows.astype(jnp.float32)
    features = inputs.shape[-1]
    head_size = queries.shape[-1]
    window_count = queries.shape[0]
    grad_out = cotangent * live_mask[:, None, None]
    branch_grad = grad_out.reshape(-1, features).astype(jnp.bfloat16)
    grad_hidden = (times_back(branch_grad, contract_mat) * gelu_slope(hidden)).astype(jnp.bfloat16)
    grad_second = times_back(grad_hidden, expand_mat).reshape(grad_out.shape)
    grad_resid = grad_out + norm_backward(grad_second * gain_rows[1], second_hat, second_inv)
    grad_attn = to_windows(grad_resid, shifted).reshape(-1, features).astype(jnp.bfloat16)
    grad_mixed = times_back(grad_attn, proj_mat).astype(jnp.bfloat16).reshape(queries.shape)
    grad_probs = jnp.einsum(
        "wihc,wjhc->whij", grad_mixed, values_in, preferred_element_type=jnp.float32
    )
    grad_values = jnp.einsum(
        "whij,wihc->wjhc", probs_low, grad_mixed, preferred_element_type=jnp.float32
    )
    grad_scores = attn_probs * (
        grad_probs - jnp.sum(grad_probs * attn_probs, axis=-1, keepdims=True)
    )
    scores_low = grad_scores.astype(jnp.bfloat16)
    grad_query = jnp.einsum(
        "whij,wjhc->wihc", scores_low, key_rows, preferred_element_type=jnp.float32
    ) * head_size ** (-0.5)
    grad_keys = jnp.einsum(
        "whij,wihc->wjhc", scores_low, queries, preferred_element_type=jnp.float32
    ) * head_size ** (-0.5)
    grad_qkv_rows = (
        jnp.stack([grad_query, grad_keys, grad_values], axis=2)
        .astype(jnp.bfloat16)
        .reshape(-1, 3 * features)
    )
    grad_blocks = times_back(grad_qkv_rows, qkv_mat)
    grad_first = from_windows(grad_blocks.reshape(window_count, WIN * WIN, features), shifted)
    grad_input = grad_resid + norm_backward(grad_first * gain_rows[0], first_hat, first_inv)
    pieces_kept = (
        saved,
        branch_grad,
        grad_hidden,
        grad_second,
        grad_attn,
        scores_low,
        grad_qkv_rows,
        grad_first,
    )
    return (grad_input, pieces_kept)


def weight_grads(pieces_kept):
    (
        saved,
        branch_grad,
        grad_hidden,
        grad_second,
        grad_attn,
        scores_low,
        grad_qkv_rows,
        grad_first,
    ) = pieces_kept
    (
        first_hat,
        first_inv,
        blocks,
        queries,
        key_rows,
        values_in,
        attn_probs,
        probs_low,
        mixed_out,
        second_hat,
        second_inv,
        second_norm,
        hidden,
        active,
    ) = saved
    features = blocks.shape[-1]
    contract_grad = inner_rows(active, branch_grad)
    out_bias_grad = jnp.sum(branch_grad, axis=0, dtype=jnp.float32)
    expand_grad = inner_rows(second_norm, grad_hidden)
    expand_bias_grad = jnp.sum(grad_hidden, axis=0, dtype=jnp.float32)
    second_gain_grad = jnp.sum(grad_second * second_hat, axis=(0, 1))
    second_shift_grad = jnp.sum(grad_second, axis=(0, 1))
    proj_grad = inner_rows(mixed_out, grad_attn)
    proj_bias_grad = jnp.sum(grad_attn, axis=0, dtype=jnp.float32)
    score_sum = jnp.sum(scores_low, axis=0, dtype=jnp.float32)
    qkv_grad = inner_rows(blocks, grad_qkv_rows)
    column_sums = jnp.sum(grad_qkv_rows, axis=0, dtype=jnp.float32)
    first_gain_grad = jnp.sum(grad_first * first_hat, axis=(0, 1))
    first_shift_grad = jnp.sum(grad_first, axis=(0, 1))
    gain_grads = jnp.stack([first_gain_grad, second_gain_grad])
    vector_grads = jnp.stack(
        [
            first_shift_grad,
            column_sums[:features],
            column_sums[2 * features :],
            proj_bias_grad,
            second_shift_grad,
            out_bias_grad,
        ]
    )
    grad_list = (
        gain_grads,
        vector_grads,
        qkv_grad,
        proj_grad,
        expand_grad,
        expand_bias_grad,
        contract_grad,
    )
    return (grad_list, score_sum)


def send_up(rows):
    return from_behind(rows, "section", 1)


def send_down(rows):
    return from_behind(rows, "section", -1)


def add_tuples(left_tuple, right_tuple):
    if left_tuple is None:
        return right_tuple
    return tuple((left_part + right_part for left_part, right_part in zip(left_tuple, right_tuple)))


def on_device(
    images,
    live_counts,
    norm_gains,
    vectors,
    qkv_weight,
    proj_weight,
    hidden_weight,
    hidden_bias,
    out_weight,
    bias_table,
    out_grad,
):
    micro_count = images.shape[0]
    slot_count = images.shape[1]
    section_index = lax.axis_index("section")
    is_first = section_index == 0
    shifted = section_index == 1
    counts = live_counts[:, 0]
    gathered = (
        lax.all_gather(norm_gains, "fsdp", axis=2, tiled=True),
        lax.all_gather(vectors, "fsdp", axis=2, tiled=True),
        lax.all_gather(qkv_weight, "fsdp", axis=1, tiled=True),
        lax.all_gather(proj_weight, "fsdp", axis=1, tiled=True),
        lax.all_gather(hidden_weight, "fsdp", axis=1, tiled=True),
        lax.all_gather(hidden_bias, "fsdp", axis=1, tiled=True),
        lax.all_gather(out_weight, "fsdp", axis=1, tiled=True),
    )
    params = tuple((member[0] for member in gathered))
    onehot = offset_onehot()
    head_count = bias_table.shape[-1]
    position_flat = jnp.dot(onehot, bias_table[0], precision=highest)
    position_bias = position_flat.T.reshape(head_count, WIN * WIN, WIN * WIN)
    region_bias = region_mask() * shifted.astype(jnp.float32)
    slot_index = jnp.arange(slot_count)
    regathered = (
        lax.all_gather(norm_gains, "fsdp", axis=2, tiled=True),
        lax.all_gather(vectors, "fsdp", axis=2, tiled=True),
        lax.all_gather(qkv_weight, "fsdp", axis=1, tiled=True),
        lax.all_gather(proj_weight, "fsdp", axis=1, tiled=True),
        lax.all_gather(hidden_weight, "fsdp", axis=1, tiled=True),
        lax.all_gather(hidden_bias, "fsdp", axis=1, tiled=True),
        lax.all_gather(out_weight, "fsdp", axis=1, tiled=True),
    )
    back_params = tuple((member[0] for member in regathered))
    kept_inputs = []
    produced = []
    saved_list = []
    input_list = []
    score_total = jnp.zeros((head_count, WIN * WIN, WIN * WIN), jnp.float32)
    shard_totals = None
    received = jnp.zeros(images.shape[1:], jnp.bfloat16)
    incoming = jnp.zeros(images.shape[1:], jnp.bfloat16)
    for moment in range(micro_count + 2):
        if moment <= micro_count:
            own_images = images[min(moment, micro_count - 1)]
            forward_inputs = jnp.where(is_first, own_images, received)
            forward_first_count = (
                counts[min(moment, micro_count - 1)] if moment < micro_count else 0
            )
            forward_second_count = counts[max(moment - 1, 0)] if moment > 0 else 0
            forward_live_count = jnp.where(is_first, forward_first_count, forward_second_count)
            forward_live_mask = (slot_index < forward_live_count).astype(jnp.float32)
            result, saved = layer_forward(
                forward_inputs, forward_live_mask, params, shifted, position_bias, region_bias
            )
            inputs, sent_rows, saved = (forward_inputs, result.astype(jnp.bfloat16), saved)
            kept_inputs.append(inputs)
            produced.append(sent_rows)
            saved_list.append(saved)
            if moment < micro_count:
                received = send_up(sent_rows)
        if moment >= 1:
            lower_at = max(moment - 2, 0)
            upper_at = min(moment, micro_count)
            upper_mb = min(moment - 1, micro_count - 1)
            cotangent = jnp.where(is_first, incoming, out_grad[upper_mb]).astype(jnp.float32)
            inputs = jnp.where(is_first, kept_inputs[lower_at], kept_inputs[upper_at])
            first_count = counts[moment - 2] if moment >= 2 else 0
            second_count = counts[moment - 1] if moment <= micro_count else 0
            live_count = jnp.where(is_first, first_count, second_count)
            live_mask = (slot_index < live_count).astype(jnp.float32)
            grad_input, pieces_kept = backward_inputs(
                inputs, live_mask, back_params, shifted, position_bias, region_bias, cotangent, None
            )
            input_list.append(grad_input)
            if moment <= micro_count:
                incoming = send_down(grad_input.astype(jnp.bfloat16))
            grad_list, score_sum = weight_grads(pieces_kept)
            score_total = score_total + score_sum
            stacked_grads = tuple((member[None] for member in grad_list))
            reduced = (
                lax.psum_scatter(stacked_grads[0], "fsdp", scatter_dimension=2, tiled=True),
                lax.psum_scatter(stacked_grads[1], "fsdp", scatter_dimension=2, tiled=True),
                lax.psum_scatter(stacked_grads[2], "fsdp", scatter_dimension=1, tiled=True),
                lax.psum_scatter(stacked_grads[3], "fsdp", scatter_dimension=1, tiled=True),
                lax.psum_scatter(stacked_grads[4], "fsdp", scatter_dimension=1, tiled=True),
                lax.psum_scatter(stacked_grads[5], "fsdp", scatter_dimension=1, tiled=True),
                lax.psum_scatter(stacked_grads[6], "fsdp", scatter_dimension=1, tiled=True),
            )
            shard_totals = add_tuples(shard_totals, reduced)
    layer_out = jnp.stack(
        [
            jnp.where(is_first, produced[index_mb], produced[index_mb + 1])
            for index_mb in range(micro_count)
        ]
    )[None]
    input_out = jnp.stack(
        [
            jnp.where(is_first, input_list[index_mb + 1], input_list[index_mb])
            for index_mb in range(micro_count)
        ]
    )[None]
    score_flat = score_total.reshape(head_count, -1).T
    table_local = lax.dot_general(onehot, score_flat, (((0,), (0,)), ((), ())), precision=highest)
    table_grad = lax.psum(table_local, "fsdp")
    return (
        layer_out,
        input_out,
        shard_totals[0],
        shard_totals[1],
        shard_totals[2],
        shard_totals[3],
        shard_totals[4],
        shard_totals[5],
        shard_totals[6],
        table_grad[None],
    )


def solution(mesh):
    in_specs = (
        P(None, "fsdp", None, None),
        P(None, "fsdp"),
        P("section", None, "fsdp"),
        P("section", None, "fsdp"),
        P("section", "fsdp", None),
        P("section", "fsdp", None),
        P("section", "fsdp", None),
        P("section", "fsdp"),
        P("section", "fsdp", None),
        P("section", None, None),
        P(None, "fsdp", None, None),
    )
    out_specs = (
        P("section", None, "fsdp", None, None),
        P("section", None, "fsdp", None, None),
        P("section", None, "fsdp"),
        P("section", None, "fsdp"),
        P("section", "fsdp", None),
        P("section", "fsdp", None),
        P("section", "fsdp", None),
        P("section", "fsdp"),
        P("section", "fsdp", None),
        P("section", None, None),
    )
    return jax.shard_map(
        on_device, mesh=mesh, in_specs=in_specs, out_specs=out_specs, check_vma=False
    )
```

profile of v0, /device:TPU:0, one launch (start us, length us, event | category | flops | bytes accessed | tf_op | source)
XLA Modules:
  0.0 2166.1 jit_solution(17052933849634913844)
XLA Ops:
  19.5 24.1 %all_gather.29 = bf16[1,6,512]{1,0,2:T(2,128)(2,1)S(1)} all-gather(bf16[1,6,32]{1,0,2:T(2,128)(2,1)S(1)} %copy.650), channel_id=1, replica_groups=mesh['section'=2,'fsdp'=16] {'fsdp'}, dimensions={2}, use_global_device_ids=true | all-gather | bytes 6528 | tf_op jit(solution)/shard_map/all_gather | solution.py:344
  43.8 11.7 slice_reduce_fusion
  55.6 18.7 all_gather.28
  83.7 18.8 all_gather.33
  106.1 19.5 all_gather.31
  136.1 11.6 reshape.1545
  147.6 6.9 fusion.996
  195.3 19.6 fusion.547
  227.5 13.7 collective-permute-done
  252.6 11.7 reshape.1546
  264.3 6.9 fusion.995
  312.7 19.4 fusion.552
  375.0 11.6 reshape.1547
  386.5 6.9 fusion.994
  437.3 19.3 fusion.557
  467.9 14.9 collective-permute-done.2
  494.7 11.6 reshape.1548
  506.2 6.9 fusion.993
  564.7 19.5 fusion.562
  596.0 14.4 collective-permute-done.3
  632.2 11.6 reshape.1549
  643.8 6.9 fusion.992
  692.3 7.9 reshape.1554
  749.4 7.9 reshape.1552
  806.3 7.9 reshape.1550
  863.5 7.9 reshape.1558
  987.6 9.9 copy.909
  997.5 13.7 copy.943
  1011.1 13.8 reshape.1534
  1046.3 11.7 reshape.1556
  1112.4 10.3 convert_element_type.971
  1159.7 18.5 fusion.191
  1178.3 7.8 convert_reduce_fusion.13
  1236.3 10.0 copy.910
  1246.2 13.7 copy.944
  1259.9 12.3 reshape.1535
  1279.0 10.3 convert_element_type.972
  1315.0 7.4 collective-permute-done.5
  1323.9 18.5 fusion.189
  1342.4 7.8 convert_reduce_fusion.12
  1400.8 9.9 copy.911
  1410.6 13.7 copy.945
  1424.3 12.4 reshape.1536
  1444.4 10.3 convert_element_type.973
  1484.2 8.1 convert_reduce_fusion.11
  1537.0 13.7 copy.946
  1550.6 12.4 reshape.1537
  1583.4 9.9 copy.912
  1593.5 10.5 convert_element_type.974
  1609.1 8.1 convert_reduce_fusion.10
  1662.3 13.7 copy.947
  1676.0 12.6 reshape.1538
  1720.5 9.9 copy.913
  1730.4 9.3 convert_element_type.975
  1745.4 18.3 fusion.187
  1770.2 18.0 fusion.185
  1788.3 18.7 add_bitcast_fusion
  1808.9 18.6 fusion.567
  1842.8 6.9 copy.916
  1850.6 57.6 %psum.7 = f32[1,169,16]{1,2,0:T(8,128)} all-reduce(f32[1,169,16]{1,2,0:T(8,128)S(1)} %fusion.580), channel_id=1, replica_groups=mesh['section'=2,'fsdp'=16] {'fsdp'}, use_global_device_ids=true, to_apply=%region_165.166 | all-reduce | flops 2704 | bytes 21632 | tf_op jit(solution)/shard_map/psum | solution.py:438
  1912.5 24.8 %reduce-scatter.16.cloned.1.call-done = f32[1,32,512]{2,1,0:T(8,128)} async-done(((f32[1,512,512]{2,1,0:T(8,128)}), f32[1,32,512]{2,1,0:T(8,128)}) %reduce-scatter.16.cloned.1.call-update) | async-done | bytes 65552 | tf_op jit(solution)/shard_map/reduce_scatter | solution.py:418
  1937.3 69.7 %reduce-scatter.14.cloned.1.call-done = f32[1,32,1536]{2,1,0:T(8,128)} async-done(((f32[1,512,1536]{2,1,0:T(8,128)}), f32[1,32,1536]{2,1,0:T(8,128)}) %reduce-scatter.14.cloned.1.call-update) | async-done | bytes 196624 | tf_op jit(solution)/shard_map/reduce_scatter | solution.py:417
  2007.0 75.9 %reduce-scatter.18.cloned.1.call-done = f32[1,32,2048]{2,1,0:T(8,128)} async-done(((f32[1,512,2048]{2,1,0:T(8,128)}), f32[1,32,2048]{2,1,0:T(8,128)}) %reduce-scatter.18.cloned.1.call-update) | async-done | bytes 262160 | tf_op jit(solution)/shard_map/reduce_scatter | solution.py:419
  2082.8 76.2 %reduce-scatter.20.cloned.1.call-done = f32[1,128,512]{2,1,0:T(8,128)} async-done(((f32[1,2048,512]{2,1,0:T(8,128)}), f32[1,128,512]{2,1,0:T(8,128)}) %reduce-scatter.20.cloned.1.call-update) | async-done | bytes 262160 | tf_op jit(solution)/shard_map/reduce_scatter | solution.py:421
  (1422 shorter events, 1092.8 us)
Async XLA Ops:
  7.2 96.4 %copy-start = (f32[1,169,16]{1,2,0:T(8,128)S(1)}, f32[1,169,16]{1,2,0:T(8,128)}, u32[]{:S(2)}) copy-start(f32[1,169,16]{1,2,0:T(8,128)} %param.20) | copy-start | bytes 32452
  7.2 124.6 %all-gather.4.cloned.1.call-start = ((), (), s32[]{:S(2)}) async-start(), calls=%async_computation.7 | async-start | bytes 1671168 | tf_op jit(solution)/shard_map/all_gather | solution.py:345
  7.9 187.3 %all-gather.6.cloned.1.call-start = ((), (), s32[]{:S(2)}) async-start(), calls=%async_computation.8 | async-start | bytes 2228224 | tf_op jit(solution)/shard_map/all_gather | solution.py:347
  8.7 186.6 %all-gather.8.cloned.1.call-start = ((), (), s32[]{:S(2)}) async-start(), calls=%async_computation.9 | async-start | bytes 2228224 | tf_op jit(solution)/shard_map/all_gather | solution.py:349
  9.4 1898.8 %reduce-scatter.22.cloned.1.call-start = ((), (), s32[]{:S(2)}) async-start(), calls=%async_computation.14 | async-start | bytes 278528
  55.6 558.3 %copy-start.259 = (f32[512]{0:T(512)}, f32[512]{0:T(512)S(1)}, u32[]{:S(2)}) copy-start(f32[512]{0:T(512)S(1)} %get-tuple-element.95) | copy-start | bytes 6148
  77.3 483.3 %copy-start.243 = (f32[512]{0:T(512)}, f32[512]{0:T(512)S(1)}, u32[]{:S(2)}) copy-start(f32[512]{0:T(512)S(1)} %get-tuple-element.96) | copy-start | bytes 6148
  77.3 536.6 %copy-start.206 = (f32[512]{0:T(512)}, f32[512]{0:T(512)S(1)}, u32[]{:S(2)}) copy-start(f32[512]{0:T(512)S(1)} %get-tuple-element.97) | copy-start | bytes 6148
  80.1 25.9 %copy-start.306 = (bf16[1,32,512]{2,1,0:T(8,128)(2,1)S(1)}, bf16[1,32,512]{2,1,0:T(8,128)(2,1)}, u32[]{:S(2)}) copy-start(bf16[1,32,512]{2,1,0:T(8,128)(2,1)} %param.16) | copy-start | bytes 98308
  103.6 25.0 %copy-start.311 = (s32[2401]{0:T(1024)}, s32[2401]{0:T(1024)S(1)}, u32[]{:S(2)}) copy-start(s32[2401]{0:T(1024)S(1)} %reshape.1503) | copy-start | bytes 28816
  220.2 21.1 collective-permute-start
  223.7 131.6 %copy-start.329 = (f32[4]{0:T(128)}, f32[4]{0:T(128)S(1)}, u32[]{:S(2)}) copy-start(f32[4]{0:T(128)S(1)} %compare_convert_fusion.4) | copy-start | bytes 52
  223.7 17.5 copy-start.162
  226.1 17.6 copy-start.92
  243.6 66.4 %copy-start.17 = (bf16[4,196,512]{2,1,0:T(8,128)(2,1)}, bf16[4,196,512]{2,1,0:T(8,128)(2,1)S(1)}, u32[]{:S(2)}) copy-start(bf16[4,196,512]{2,1,0:T(8,128)(2,1)S(1)} %get-tuple-element.154) | copy-start | bytes 2408452
  338.2 20.0 copy-start.133
  340.5 22.3 %collective-permute-start.1 = (bf16[4,196,512]{2,0,1:T(4,128)(2,1)}, bf16[4,196,512]{2,0,1:T(4,128)(2,1)}, u32[]{:S(2)}, u32[]{:S(2)}) collective-permute-start(bf16[4,196,512]{2,0,1:T(4,128)(2,1)} %copy.688), channel_id=1, source_target_pairs={{0,16},{1,17},{2,18},{3,19},{4,20},{5,21},{6,22},{7,23},{8,24},{9,... | collective-permute-start | bytes 2408456 | tf_op jit(solution)/shard_map/ppermute | solution.py:21
  365.1 69.5 %copy-start.25 = (bf16[4,196,512]{2,1,0:T(8,128)(2,1)}, bf16[4,196,512]{2,1,0:T(8,128)(2,1)S(1)}, u32[]{:S(2)}) copy-start(bf16[4,196,512]{2,1,0:T(8,128)(2,1)S(1)} %get-tuple-element.159) | copy-start | bytes 2408452
  365.1 248.8 %copy-start.11 = (bf16[4,196,512]{2,1,0:T(8,128)(2,1)}, bf16[4,196,512]{2,1,0:T(8,128)(2,1)S(1)}, u32[]{:S(2)}) copy-start(bf16[4,196,512]{2,1,0:T(8,128)(2,1)S(1)} %get-tuple-element.158) | copy-start | bytes 2408452
  459.4 23.4 %copy-start.18 = (bf16[4,196,512]{2,1,0:T(8,128)(2,1)S(1)}, bf16[4,196,512]{2,1,0:T(8,128)(2,1)}, u32[]{:S(2)}) copy-start(bf16[4,196,512]{2,1,0:T(8,128)(2,1)} %copy-done.17) | copy-start | bytes 2408452
  459.4 23.4 %copy-start.122 = (bf16[1,4,196,512]{3,1,2,0:T(4,128)(2,1)S(1)}, bf16[1,4,196,512]{3,1,2,0:T(4,128)(2,1)}, u32[]{:S(2)}) copy-start(bf16[1,4,196,512]{3,1,2,0:T(4,128)(2,1)} %get-tuple-element.219) | copy-start | bytes 2408452
  463.1 20.3 copy-start.106
  463.5 19.3 collective-permute-start.2
  466.9 147.0 %copy-start.246 = (f32[4,196]{1,0:T(4,128)}, f32[4,196]{1,0:T(4,128)S(1)}, u32[]{:S(2)}) copy-start(f32[4,196]{1,0:T(4,128)S(1)} %broadcast_multiply_fusion.29) | copy-start | bytes 9412
  467.4 146.5 %copy-start.268 = (f32[4,196]{1,0:T(4,128)}, f32[4,196]{1,0:T(4,128)S(1)}, u32[]{:S(2)}) copy-start(f32[4,196]{1,0:T(4,128)S(1)} %add_rsqrt_fusion.9) | copy-start | bytes 9412
  467.4 146.5 %copy-start.266 = (f32[4,196]{1,0:T(4,128)}, f32[4,196]{1,0:T(4,128)S(1)}, u32[]{:S(2)}) copy-start(f32[4,196]{1,0:T(4,128)S(1)} %broadcast_multiply_fusion.24) | copy-start | bytes 9412
  483.4 130.5 %copy-start.8 = (bf16[4,196,512]{2,1,0:T(8,128)(2,1)}, bf16[4,196,512]{2,1,0:T(8,128)(2,1)S(1)}, u32[]{:S(2)}) copy-start(bf16[4,196,512]{2,1,0:T(8,128)(2,1)S(1)} %get-tuple-element.163) | copy-start | bytes 2408452
  587.0 23.4 %copy-start.16 = (bf16[4,196,512]{2,1,0:T(8,128)(2,1)S(1)}, bf16[4,196,512]{2,1,0:T(8,128)(2,1)}, u32[]{:S(2)}) copy-start(bf16[4,196,512]{2,1,0:T(8,128)(2,1)} %copy-done.14) | copy-start | bytes 2408452
  587.0 23.4 %copy-start.123 = (bf16[1,4,196,512]{3,1,2,0:T(4,128)(2,1)S(1)}, bf16[1,4,196,512]{3,1,2,0:T(4,128)(2,1)}, u32[]{:S(2)}) copy-start(bf16[1,4,196,512]{3,1,2,0:T(4,128)(2,1)} %get-tuple-element.219) | copy-start | bytes 2408452
  591.3 19.1 collective-permute-start.3
  595.5 18.5 copy-start.290
  595.5 18.5 copy-start.264
  595.5 16.3 copy-start.26
  596.0 18.0 copy-start.288
  1011.1 13.8 copy-start.356
  1109.8 25.9 %copy-start.140 = (bf16[784,512]{1,0:T(8,128)(2,1)}, bf16[784,512]{1,0:T(8,128)(2,1)S(1)}, u32[]{:S(2)}) copy-start(bf16[784,512]{1,0:T(8,128)(2,1)S(1)} %reshape.1466) | copy-start | bytes 2408452
  1129.6 27.5 %collective-permute-start.4 = (bf16[4,196,512]{2,0,1:T(4,128)(2,1)}, bf16[4,196,512]{2,0,1:T(4,128)(2,1)}, u32[]{:S(2)}, u32[]{:S(2)}) collective-permute-start(bf16[4,196,512]{2,0,1:T(4,128)(2,1)} %copy.770), channel_id=1, source_target_pairs={{16,0},{17,1},{18,2},{19,3},{20,4},{21,5},{22,6},{23,7},{24,8},{25... | collective-permute-start | bytes 2408456 | tf_op jit(solution)/shard_map/ppermute | solution.py:21
  1159.7 18.5 copy-start.215
  1159.7 18.5 copy-start.354
  1303.8 18.7 collective-permute-start.5
  1309.3 13.2 copy-start.120
  1309.3 13.2 copy-start.336
  1323.9 18.5 copy-start.216
  1323.9 18.5 copy-start.355
  1465.2 17.5 collective-permute-start.6
  1579.9 27.3 %collective-permute-start.7 = (bf16[4,196,512]{2,0,1:T(4,128)(2,1)}, bf16[4,196,512]{2,0,1:T(4,128)(2,1)}, u32[]{:S(2)}, u32[]{:S(2)}) collective-permute-start(bf16[4,196,512]{2,0,1:T(4,128)(2,1)} %copy.875), channel_id=1, source_target_pairs={{16,0},{17,1},{18,2},{19,3},{20,4},{21,5},{22,6},{23,7},{24,8},{25... | collective-permute-start | bytes 2408456 | tf_op jit(solution)/shard_map/ppermute | solution.py:21
  1701.1 208.5 %reduce-scatter.26.cloned.1.call-start = ((), (), s32[]{:S(2)}) async-start(), calls=%async_computation.16 | async-start | bytes 1114112
  1703.5 207.5 %reduce-scatter.24.cloned.1.call-start = ((), (), s32[]{:S(2)}) async-start(), calls=%async_computation.15 | async-start | bytes 278528
  1704.9 232.4 %reduce-scatter.16.cloned.1.call-start = ((), (), s32[]{:S(2)}) async-start(), calls=%async_computation.11 | async-start | bytes 1114112 | tf_op jit(solution)/shard_map/reduce_scatter | solution.py:418
  1708.2 298.8 %reduce-scatter.14.cloned.1.call-start = ((), (), s32[]{:S(2)}) async-start(), calls=%async_computation.10 | async-start | bytes 3342336 | tf_op jit(solution)/shard_map/reduce_scatter | solution.py:417
  1745.3 18.4 copy-start.169
  1745.3 337.5 %reduce-scatter.18.cloned.1.call-start = ((), (), s32[]{:S(2)}) async-start(), calls=%async_computation.12 | async-start | bytes 4456448 | tf_op jit(solution)/shard_map/reduce_scatter | solution.py:419
  1745.4 18.4 copy-start.68
  1745.4 18.4 copy-start.69
  1745.4 18.4 copy-start.70
  1745.4 18.4 copy-start.71
  1745.4 18.4 copy-start.95
  1769.1 19.2 copy-start.197
  1769.1 19.2 copy-start.331
  1769.1 389.9 %reduce-scatter.20.cloned.1.call-start = ((), (), s32[]{:S(2)}) async-start(), calls=%async_computation.13 | async-start | bytes 4456448 | tf_op jit(solution)/shard_map/reduce_scatter | solution.py:421
  1770.2 18.1 copy-start.359
  1770.2 18.1 copy-start.360
  1770.2 18.1 copy-start.361
  1842.8 316.2 %copy-start.1 = (f32[1,169,16]{1,2,0:T(8,128)S(1)}, f32[1,169,16]{1,2,0:T(8,128)}, u32[]{:S(2)}) copy-start(f32[1,169,16]{1,2,0:T(8,128)} %param.20) | copy-start | bytes 32452
  (330 other events, 1387.8 us)
Sparse Core Ops, SparseCore 0:
  10.3 42.4 all-gather.3
  55.0 40.6 all-gather.5
  97.8 40.5 all-gather.7
  1701.2 56.8 reduce-scatter.21
  1761.6 56.4 reduce-scatter.25
  1821.9 54.2 reduce-scatter.23
  1880.8 56.4 reduce-scatter.15
  1941.7 65.2 reduce-scatter.13
  2011.4 71.3 reduce-scatter.17
  2087.6 71.3 reduce-scatter.19
where the time goes:
time: 2180 us; the launch traced here: 2170 us
  local copies, waits for them, and re-layouts  897 us (41%)
  matrix products  558 us (26%)
  waiting for transfers between devices  304 us (14%)
  other arithmetic  213 us (10%)
  blocking collectives  139 us (6%)
  between operations  31 us (1%)
  starting transfers between devices  23.5 us (1%)
    unnamed x794, local copies, waits for them, and re-layouts  217 us
    convert_element_type x15, local copies, waits for them, and re-layouts, backward_inputs(): grad_qkv_rows = jnp.stack([grad_query, grad_keys, grad_values], axis=2).a...  182 us
    dot_general x20, matrix products, inner_rows(): lax.dot_general(left_rows, right_rows, (((0,), (0,)), ((), ())), preferre...  160 us
    reshape x10, local copies, waits for them, and re-layouts, layer_forward(): projected.reshape(window_count, WIN * WIN, 3, head_count, head_size)  101 us
    dot_general x5, matrix products, layer_forward(): jnp.dot(active, contract_mat, preferred_element_type=jnp.float32)  96.4 us
    dot_general x20, matrix products, times_back(): lax.dot_general(left_rows, matrix, (((1,), (1,)), ((), ())), preferred_el...  83.8 us
    reduce_scatter x1, waiting for transfers between devices, on_device(): lax.psum_scatter(stacked_grads[6], 'fsdp', scatter_dimension=1, tiled=True)  76.2 us
    reduce_scatter x1, waiting for transfers between devices, on_device(): lax.psum_scatter(stacked_grads[4], 'fsdp', scatter_dimension=1, tiled=True)  75.9 us
  transfers between devices with their start and end apart: 18, of which 9 were waited for; matrix products, arithmetic and copies ran while one was open for 15% of the time, Pallas kernels for 0%

commit v1 on v0

v1 whole, which is shorter than its diff:
```python
import functools
import math

import jax
import jax.numpy as jnp
import numpy as np
from jax import lax
from jax.experimental import pallas as pl
from jax.experimental.pallas import tpu as pltpu
from jax.sharding import PartitionSpec as P

WIN = 7
GRID = 14
SHIFT = 3
TABLE = 169
HEADS = 16
HEAD = 32
D = 512
FF = 2048
TOK = 196
PAD = 208
PAIR = 2
BOTH = PAIR * PAD
WTOK = 64
WINS = 4
ALL = WINS * WTOK
GROUP = 4
GROUPS = HEADS // GROUP
CH = FF // D
BLOCKS = 16
ROWS = D // BLOCKS
QKV_AT, PROJ_AT, HID_AT, OUT_AT, SMALL_AT = 0, 96, 128, 256, 384
PACK_ROWS = 400
GRAD_ROWS = 416
EPS = 1e-05
LOG2E = 1.4426950408889634
SCALE = HEAD**-0.5
LOWEST = -1e30
LIST = 8
VMEM_LIMIT = 60 * 1024 * 1024
SHARDED = ("chip", "core")
SWAP = [(0, 1), (1, 0)]

bf16 = jnp.bfloat16
f32 = jnp.float32


def window_places():
    tables = []
    for shift in (0, SHIFT):
        table = np.full((ALL,), -1, np.int64)
        for window in range(WINS):
            for r in range(WIN):
                for c in range(WIN):
                    row = ((window // 2) * WIN + r + shift) % GRID
                    column = ((window % 2) * WIN + c + shift) % GRID
                    table[window * WTOK + 8 * r + c] = row * GRID + column
        tables.append(table)
    return tables


def permutations():
    mats = []
    for table in window_places():
        mat = np.zeros((ALL, PAD), np.float32)
        for at, token in enumerate(table):
            if token >= 0:
                mat[at, token] = 1.0
        mats.append(mat)
    return mats


def pair_offsets():
    place = np.arange(WTOK)
    r, c = place // 8, place % 8
    real = (r < WIN) & (c < WIN)
    offset = (r[None, :] - r[:, None] + WIN - 1) * (2 * WIN - 1) + c[None, :] - c[:, None] + WIN - 1
    return np.where(real[None, :] & real[:, None], offset, -1)


def region_masks():
    line = np.arange(GRID)
    band = (line >= GRID - WIN).astype(int) + (line >= GRID - SHIFT).astype(int)
    out = np.zeros((WINS, WTOK, WTOK), np.float32)
    for window in range(WINS):
        ids = np.full((WTOK,), -1)
        for r in range(WIN):
            for c in range(WIN):
                ids[8 * r + c] = (
                    3 * band[(window // 2) * WIN + r] + band[(window % 2) * WIN + c]
                )
        out[window] = np.where(ids[:, None] != ids[None, :], -100.0, 0.0)
    return out


def bias_arrays(table, masked):
    offsets = pair_offsets()
    pick = jnp.asarray(offsets.reshape(-1, 1), jnp.int32) == jnp.arange(TABLE, dtype=jnp.int32)[None, :]
    flat = jnp.dot(pick.astype(f32), table, precision=lax.Precision.HIGHEST)
    bias = flat.reshape(WTOK, WTOK, GROUPS, GROUP).transpose(2, 0, 3, 1)
    if masked:
        bias = bias[None] + jnp.asarray(region_masks())[:, None, :, None, :]
    else:
        bias = bias[None]
    place = np.arange(WTOK)
    real_key = (place // 8 < WIN) & (place % 8 < WIN)
    bias = jnp.where(jnp.asarray(real_key)[None, None, :, None, None], bias * LOG2E, LOWEST)
    return bias.reshape(bias.shape[0], GROUPS, WTOK, GROUP * WTOK)


def dot(a, b):
    return jnp.dot(a, b, preferred_element_type=f32)


def dot_nt(a, b):
    return lax.dot_general(a, b, (((1,), (1,)), ((), ())), preferred_element_type=f32)


def dot_tn(a, b):
    return lax.dot_general(a, b, (((0,), (0,)), ((), ())), preferred_element_type=f32)


def block(w_ref, at):
    return w_ref[:, pl.ds(at, ROWS), :].reshape(D, D)


def out_block(w_ref, k):
    return w_ref[pl.ds(k * (BLOCKS // CH), BLOCKS // CH), OUT_AT:SMALL_AT, :].reshape(D, D)


def normalize(values):
    center = values - jnp.mean(values, axis=-1, keepdims=True)
    inverse = lax.rsqrt(jnp.mean(center * center, axis=-1, keepdims=True) + EPS)
    return center * inverse, inverse


def norm_backward(grad_hat, hat, inverse):
    mean = jnp.mean(grad_hat, axis=-1, keepdims=True)
    along = jnp.mean(grad_hat * hat, axis=-1, keepdims=True)
    return inverse * (grad_hat - mean - hat * along)


ERF_T = 0.3275911
ERF_C = (0.254829592, -0.284496736, 1.421413741, -1.453152027, 1.061405429)


def gelu_and_slope(u):
    u = u.astype(bf16)
    size = jnp.abs(u)
    t = pltpu.reciprocal(size * bf16(ERF_T * 0.5**0.5) + bf16(1.0), approx=True)
    bell = jnp.exp2(u * u * bf16(-0.5 * LOG2E))
    tail = bf16(0.5 * ERF_C[4])
    for c in ERF_C[3::-1]:
        tail = tail * t + bf16(0.5 * c)
    tail = tail * t * bell
    phi = jnp.where(u >= bf16(0.0), bf16(1.0) - tail, tail)
    return jnp.maximum(u, bf16(0.0)) - size * tail, phi + u * bell * bf16((0.5 / math.pi) ** 0.5)


def head_masks():
    lane_head = lax.broadcasted_iota(jnp.int32, (WTOK, GROUP * HEAD), 1) // HEAD
    return [(lane_head == h).astype(f32).astype(bf16) for h in range(GROUP)]


def spread_heads(tile, masks):
    return jnp.concatenate([tile * mask for mask in masks], axis=0)


def put_diagonal(out_ref, image, group, pair, even, odd):
    for h in range(GROUP):
        rows, lanes = slice(h * HEAD, (h + 1) * HEAD), slice(h * WTOK, (h + 1) * WTOK)
        both = jnp.concatenate([even[rows, lanes], odd[rows, lanes]], axis=1)
        at = group * GROUP * HEAD + h * HEAD
        out_ref[image, at : at + HEAD, pair * 128 : (pair + 1) * 128] = both.astype(bf16)


def tiles_of(pair, group):
    lanes = slice(group * GROUP * HEAD, (group + 1) * GROUP * HEAD)
    for image in range(PAIR):
        for window in (2 * pair, 2 * pair + 1):
            at = image * ALL + window * WTOK
            yield image, window, slice(at, at + WTOK), lanes


def attention_forward(q_ref, k_ref, v_ref, p_ref, ot_ref, bias_ref):
    masks = head_masks()
    bias_windows = bias_ref.shape[0]
    for pair in range(WINS // 2):
        for group in range(GROUPS):
            tiles = list(tiles_of(pair, group))
            scores = [
                dot_nt(k_ref[rows, lanes], spread_heads(q_ref[rows, lanes], masks)) * (SCALE * LOG2E)
                + bias_ref[window if bias_windows > 1 else 0, group]
                for _, window, rows, lanes in tiles
            ]
            tops = [jnp.max(tile, axis=0, keepdims=True) for tile in scores]
            powers = [jnp.exp2(tile - top) for tile, top in zip(scores, tops)]
            totals = [1.0 / jnp.sum(tile, axis=0, keepdims=True) for tile in powers]
            probs = [(tile * total).astype(bf16) for tile, total in zip(powers, totals)]
            for (image, window, _, _), tile in zip(tiles, probs):
                p_ref[image, window, group] = tile
            products = [
                dot_tn(v_ref[rows, lanes], tile) for (_, _, rows, lanes), tile in zip(tiles, probs)
            ]
            for image in range(PAIR):
                put_diagonal(ot_ref, image, group, pair, *products[2 * image : 2 * image + 2])


def attention_backward(q_ref, k_ref, v_ref, p_ref, do_ref, dqt_ref, dk_ref, dv_ref, score_ref):
    masks = head_masks()
    for pair in range(WINS // 2):
        for group in range(GROUPS):
            tiles = list(tiles_of(pair, group))
            spreads = [spread_heads(do_ref[rows, lanes], masks) for _, _, rows, lanes in tiles]
            probs = [p_ref[image, window, group] for image, window, _, _ in tiles]
            grad_probs = [
                dot_nt(v_ref[rows, lanes], spread) for (_, _, rows, lanes), spread in zip(tiles, spreads)
            ]
            for (_, _, rows, lanes), tile, spread in zip(tiles, probs, spreads):
                dv_ref[rows, lanes] = dot(tile, spread).astype(bf16)
            weighted = [tile * prob.astype(f32) for tile, prob in zip(grad_probs, probs)]
            sums = [jnp.sum(tile, axis=0, keepdims=True) for tile in weighted]
            grads = [
                tile - prob.astype(f32) * total for tile, prob, total in zip(weighted, probs, sums)
            ]
            score_ref[group] += (grads[0] + grads[1]) + (grads[2] + grads[3])
            lows = [tile.astype(bf16) for tile in grads]
            for (_, _, rows, lanes), low in zip(tiles, lows):
                queries = spread_heads(q_ref[rows, lanes], masks)
                dk_ref[rows, lanes] = (dot(low, queries) * SCALE).astype(bf16)
            products = [
                dot_tn(k_ref[rows, lanes], low) * SCALE for (_, _, rows, lanes), low in zip(tiles, lows)
            ]
            for image in range(PAIR):
                put_diagonal(dqt_ref, image, group, pair, *products[2 * image : 2 * image + 2])


def to_windows(perm_ref, rows):
    return jnp.concatenate(
        [dot(perm_ref[...], rows[i * PAD : (i + 1) * PAD]).astype(bf16) for i in range(PAIR)], axis=0
    )


def from_windows(perm_t_ref, ref):
    return jnp.concatenate(
        [dot(perm_t_ref[...], ref[i * ALL : (i + 1) * ALL, :]) for i in range(PAIR)], axis=0
    )


def from_windows_turned(perm_t_ref, ref):
    return jnp.concatenate([dot_nt(perm_t_ref[...], ref[i]) for i in range(PAIR)], axis=0)


def forward_part(x_ref, w_ref, small_ref, perm_ref, perm_t_ref, bias_ref, a):
    hat1, inv1 = normalize(x_ref[...])
    norm1 = (hat1 * small_ref[0:1, :] + small_ref[2:3, :]).astype(bf16)
    blocks = to_windows(perm_ref, norm1)
    a["q"][...] = (dot(blocks, block(w_ref, QKV_AT)) + small_ref[3:4, :]).astype(bf16)
    a["k"][...] = dot(blocks, block(w_ref, QKV_AT + ROWS)).astype(bf16)
    a["v"][...] = (dot(blocks, block(w_ref, QKV_AT + 2 * ROWS)) + small_ref[4:5, :]).astype(bf16)
    attention_forward(a["q"], a["k"], a["v"], a["p"], a["ot"], bias_ref)
    mixed = from_windows_turned(perm_t_ref, a["ot"]).astype(bf16)
    resid = x_ref[...] + dot(mixed, block(w_ref, PROJ_AT)) + small_ref[5:6, :]
    a["resid"][...] = resid
    hat2, inv2 = normalize(resid)
    norm2 = (hat2 * small_ref[1:2, :] + small_ref[6:7, :]).astype(bf16)
    a["n2"][...] = norm2
    a["h"][...] = resid + small_ref[7:8, :]

    def chunk(k):
        hidden = dot(a["n2"][...], block(w_ref, HID_AT + k * ROWS)) + small_ref[pl.ds(8 + k, 1), :]
        active, slope = gelu_and_slope(hidden)
        a["g"][k] = active
        a["slope"][k] = slope
        a["h"][...] += dot(active, out_block(w_ref, k))

    for k in range(CH):
        chunk(k)
    return hat1, inv1, norm1, hat2, inv2


def add_rows(ref, at, values):
    ref[at] += jnp.sum(values.reshape(BOTH // 8, 8, D), axis=0)


def backward_part(e_ref, hats, w_ref, small_ref, perm_ref, perm_t_ref, a, b):
    hat1, inv1, norm1, hat2, inv2 = hats

    def back(rows, at):
        if at < 4 + CH:
            return dot_nt(rows, block(w_ref, at * ROWS))
        return dot_nt(rows, out_block(w_ref, at - 4 - CH))

    out_grad = e_ref[...].astype(bf16)
    add_rows(b["rows"], 7, out_grad.astype(f32))
    b["dz"][...] = out_grad
    b["dzt"][...] = out_grad.T
    b["n2t"][...] = a["n2"][...].T
    b["dn2"][...] = jnp.zeros((BOTH, D), f32)

    def chunk(k):
        grad_hidden = back(b["dz"][...], 4 + CH + k) * a["slope"][k].astype(f32)
        b["rows"][8 + k] += jnp.sum(grad_hidden.reshape(BOTH // 8, 8, D), axis=0)
        low = grad_hidden.astype(bf16)
        b["dn2"][...] += back(low, 4 + k)
        at = pl.ds(HID_AT + k * ROWS, ROWS)
        b["acc"][:, at, :] += dot(b["n2t"][...], low).reshape(BLOCKS, ROWS, D)
        b["acc_out"][k] += dot(b["dzt"][...], a["g"][k])

    for k in range(CH):
        chunk(k)
    dn2 = b["dn2"][...]
    add_rows(b["rows"], 1, dn2 * hat2)
    add_rows(b["rows"], 6, dn2)
    dr = e_ref[...] + norm_backward(dn2 * small_ref[1:2, :], hat2, inv2)
    low = dr.astype(bf16)
    add_rows(b["rows"], 5, low.astype(f32))
    attn = to_windows(perm_ref, low)
    b["do"][...] = back(attn, 3).astype(bf16)
    proj = dot(a["ot"][0], attn[:ALL]) + dot(a["ot"][1], attn[ALL:])
    b["acc"][:, PROJ_AT : PROJ_AT + ROWS, :] += proj.reshape(BLOCKS, ROWS, D)
    attention_backward(
        a["q"], a["k"], a["v"], a["p"], b["do"], b["dqt"], b["dk"], b["dv"], b["scores"]
    )
    norm1_t = norm1.T
    dn1 = jnp.zeros((BOTH, D), f32)
    for at in range(3):
        if at == 0:
            rows = from_windows_turned(perm_t_ref, b["dqt"])
        else:
            rows = from_windows(perm_t_ref, b["dk" if at == 1 else "dv"])
        if at != 1:
            add_rows(b["rows"], 3 + at // 2, rows)
        rows = rows.astype(bf16)
        dn1 = dn1 + back(rows, at)
        take = slice(QKV_AT + at * ROWS, QKV_AT + (at + 1) * ROWS)
        b["acc"][:, take, :] += dot(norm1_t, rows).reshape(BLOCKS, ROWS, D)
    add_rows(b["rows"], 0, dn1 * hat1)
    add_rows(b["rows"], 2, dn1)
    return dr + norm_backward(dn1 * small_ref[0:1, :], hat1, inv1)


def clear_sums(b):
    for name in ("acc", "acc_out", "rows", "scores"):
        b[name][...] = jnp.zeros(b[name].shape, f32)


def table_rows(score_ref, fold_ref):
    lane = lax.broadcasted_iota(jnp.int32, (WTOK, 128), 1)
    for head in range(HEADS):
        group, h = head // GROUP, head % GROUP
        tile = score_ref[group, :, 128 * (h // 2) : 128 * (h // 2) + 128]
        if h % 2:
            tile = pltpu.roll(tile, WTOK, 1)
        tile = jnp.where(lane < WTOK, tile, 0.0)
        total = jnp.zeros((8, 128), f32)
        for r in range(WIN):
            turned = tile[8 * r : 8 * r + 8]
            if r < WIN - 1:
                turned = pltpu.roll(turned, 8 * (WIN - 1 - r), 1)
            total = total + turned
        fold_ref[8 * head : 8 * head + 8, :] = total
    lane = lax.broadcasted_iota(jnp.int32, (128, 256), 0)
    goal = lax.broadcasted_iota(jnp.int32, (128, 256), 1)
    out = jnp.zeros((HEADS, 256), f32)
    for c in range(WIN):
        pick = (goal == 16 * (lane // 8) + lane % 8 - c + WIN - 1) & (lane % 8 < WIN)
        out = out + jnp.dot(
            fold_ref[pl.ds(c, HEADS, stride=8), :],
            pick.astype(f32),
            precision=lax.Precision.HIGHEST,
            preferred_element_type=f32,
        )
    return out


def write_sums(b, fold_ref, put):
    everything = slice(0, D)
    width = FF // BLOCKS
    for owner in range(BLOCKS):
        k, lane = owner // (BLOCKS // CH), width * (owner % (BLOCKS // CH))
        put(owner, slice(0, OUT_AT), everything, lambda: b["acc"][owner].astype(bf16))
        for at in range(D // width):
            lanes = slice(at * width, (at + 1) * width)
            put(
                owner,
                slice(OUT_AT, SMALL_AT),
                lanes,
                lambda: b["acc_out"][k, lanes, lane : lane + width].astype(bf16),
            )
    rows = jnp.sum(b["rows"][...], axis=1)
    rows = jnp.concatenate([rows, jnp.zeros((4, D), f32)], axis=0).astype(bf16)
    table = table_rows(b["scores"], fold_ref)
    table = jnp.concatenate([table, jnp.zeros((HEADS, D - 256), f32)], axis=1).astype(bf16)
    for owner in range(BLOCKS):
        put(owner, slice(SMALL_AT, PACK_ROWS), everything, lambda: rows)
        put(owner, slice(PACK_ROWS, GRAD_ROWS), everything, lambda: table)


def sum_small(w_ref, small_ref):
    small_ref[...] = jnp.sum(w_ref[:, SMALL_AT:PACK_ROWS, :].astype(f32), axis=0)


KEPT = {
    "q": ((PAIR * ALL, D), bf16),
    "k": ((PAIR * ALL, D), bf16),
    "v": ((PAIR * ALL, D), bf16),
    "p": ((PAIR, WINS, GROUPS, WTOK, GROUP * WTOK), bf16),
    "ot": ((PAIR, D, ALL), bf16),
    "resid": ((BOTH, D), f32),
    "g": ((CH, BOTH, D), bf16),
    "slope": ((CH, BOTH, D), bf16),
}
LOCAL_F = {"n2": ((BOTH, D), bf16), "h": ((BOTH, D), f32)}
LOCAL_B = {
    "acc": ((BLOCKS, OUT_AT, D), f32),
    "acc_out": ((CH, D, D), f32),
    "rows": ((12, 8, D), f32),
    "scores": ((GROUPS, WTOK, GROUP * WTOK), f32),
    "dz": ((BOTH, D), bf16),
    "dzt": ((D, BOTH), bf16),
    "n2t": ((D, BOTH), bf16),
    "dn2": ((BOTH, D), f32),
    "do": ((PAIR * ALL, D), bf16),
    "dqt": ((PAIR, D, ALL), bf16),
    "dk": ((PAIR * ALL, D), bf16),
    "dv": ((PAIR * ALL, D), bf16),
}


def scratch(shapes):
    return [pltpu.VMEM(shape, dtype) for shape, dtype in shapes.values()]


def load_images(goal_ref, where_ref, step, refs):
    for image in range(PAIR):
        at = PAIR * step + image
        rows = slice(image * PAD, image * PAD + TOK)
        for core in range(2):

            @pl.when((at < where_ref[0]) & (where_ref[1 + at] // where_ref[1 + LIST] == core))
            def _():
                goal_ref[rows, :] = refs[2 * image + core][0, 0].astype(f32)

        @pl.when(at >= where_ref[0])
        def _():
            goal_ref[rows, :] = jnp.zeros((TOK, D), f32)


def load_rows(goal_ref, ref):
    for image in range(PAIR):
        goal_ref[image * PAD : image * PAD + TOK, :] = ref[image, 0:TOK, :].astype(f32)


def store_sides(own_ref, send_ref, where_ref, first, second):
    for section in range(2):

        @pl.when(where_ref[4 + LIST] == section)
        def _():
            own_ref[...] = second if section else first
            send_ref[...] = first if section else second


def store_rows(ref, values):
    for image in range(PAIR):
        ref[image] = values[image * PAD : (image + 1) * PAD].astype(bf16)


def first_kernel(where_ref, x0, x1, x2, x3, w_ref, perm_ref, perm_t_ref, bias_ref, h_ref, *refs):
    kept = dict(zip(KEPT, refs))
    refs = refs[len(KEPT) :]
    kept.update(zip(LOCAL_F, refs))
    xs_ref, small_ref = refs[len(LOCAL_F) :]
    kept = {name: (ref.at[0] if name in KEPT else ref) for name, ref in kept.items()}
    step = pl.program_id(0)

    @pl.when(step == 0)
    def _():
        xs_ref[...] = jnp.zeros(xs_ref.shape, f32)
        sum_small(w_ref, small_ref)

    @pl.when(PAIR * step < where_ref[0])
    def _():
        load_images(xs_ref, where_ref, step, (x0, x1, x2, x3))
        forward_part(xs_ref, w_ref, small_ref, perm_ref, perm_t_ref, bias_ref, kept)
        store_rows(h_ref, kept["h"][...])


def second_kernel(
    where_ref,
    x_ref,
    e0,
    e1,
    e2,
    e3,
    w_ref,
    perm_ref,
    perm_t_ref,
    bias_ref,
    own_ref,
    send_ref,
    ig_ref,
    gp_ref,
    *refs,
):
    names = {**KEPT, **LOCAL_F}
    kept = dict(zip(names, refs))
    refs = refs[len(names) :]
    sums = dict(zip(LOCAL_B, refs))
    xs_ref, es_ref, small_ref, fold_ref = refs[len(LOCAL_B) :]
    step = pl.program_id(0)

    @pl.when(step == 0)
    def _():
        xs_ref[...] = jnp.zeros(xs_ref.shape, f32)
        es_ref[...] = jnp.zeros(es_ref.shape, f32)
        sum_small(w_ref, small_ref)
        clear_sums(sums)

    @pl.when(PAIR * step < where_ref[0])
    def _():
        load_rows(xs_ref, x_ref)
        load_images(es_ref, where_ref, step, (e0, e1, e2, e3))
        hats = forward_part(xs_ref, w_ref, small_ref, perm_ref, perm_t_ref, bias_ref, kept)
        out = kept["h"][...].reshape(PAIR, PAD, D).astype(bf16)
        store_sides(own_ref, send_ref, where_ref, x_ref[...], out)
        grad = backward_part(es_ref, hats, w_ref, small_ref, perm_ref, perm_t_ref, kept, sums)
        store_rows(ig_ref, grad)

    @pl.when(step == pl.num_programs(0) - 1)
    def _():
        def put(owner, rows, lanes, values):
            gp_ref[owner, rows, lanes] = values()

        write_sums(sums, fold_ref, put)


def third_kernel(where_ref, x0, x1, x2, x3, e_ref, w_ref, perm_ref, perm_t_ref, *refs):
    kept = {name: ref.at[0] for name, ref in zip(KEPT, refs)}
    own_ref, other_ref, keep_ref, send_ref = refs[len(KEPT) : len(KEPT) + 4]
    refs = refs[len(KEPT) + 4 :]
    sums = dict(zip(LOCAL_B, refs))
    n2_ref, xs_ref, es_ref, small_ref, fold_ref = refs[len(LOCAL_B) :]
    kept["n2"] = n2_ref
    step = pl.program_id(0)

    @pl.when(step == 0)
    def _():
        xs_ref[...] = jnp.zeros(xs_ref.shape, f32)
        es_ref[...] = jnp.zeros(es_ref.shape, f32)
        sum_small(w_ref, small_ref)
        clear_sums(sums)

    @pl.when(PAIR * step < where_ref[0])
    def _():
        load_images(xs_ref, where_ref, step, (x0, x1, x2, x3))
        load_rows(es_ref, e_ref)
        hat1, inv1 = normalize(xs_ref[...])
        norm1 = (hat1 * small_ref[0:1, :] + small_ref[2:3, :]).astype(bf16)
        hat2, inv2 = normalize(kept["resid"][...])
        n2_ref[...] = (hat2 * small_ref[1:2, :] + small_ref[6:7, :]).astype(bf16)
        hats = (hat1, inv1, norm1, hat2, inv2)
        grad = backward_part(es_ref, hats, w_ref, small_ref, perm_ref, perm_t_ref, kept, sums)
        out = grad.reshape(PAIR, PAD, D).astype(bf16)
        store_sides(own_ref, other_ref, where_ref, out, e_ref[...])

    @pl.when(step == pl.num_programs(0) - 1)
    def _():
        for core in range(2):

            @pl.when(where_ref[2 + LIST] == core)
            def _():
                def put(owner, rows, lanes, values):
                    goal_ref = keep_ref if owner % 2 == core else send_ref
                    goal_ref[owner // 2, rows, lanes] = values()

                write_sums(sums, fold_ref, put)


def spread_kernel(flags_ref, *refs):
    out_ref, held_ref = refs[-2:]
    slots = out_ref.shape[2]
    for slot in range(slots):
        kind = flags_ref[pl.program_id(0) * slots + slot]
        for at in range(4):

            @pl.when(kind == at)
            def _():
                held_ref[slot] = refs[4 * slot + at][0]

        @pl.when(kind == 4)
        def _():
            held_ref[slot] = jnp.zeros(held_ref.shape[1:], held_ref.dtype)

    values = [held_ref[slot, 0:TOK, :].astype(out_ref.dtype) for slot in range(slots)]
    if out_ref.dtype == f32:
        for slot in range(slots):
            out_ref[0, :, slot, :] = values[slot]
    else:
        out_ref[0] = jnp.stack(values, axis=1)


def whole(array):
    zeros = (0,) * array.ndim
    return pl.BlockSpec(array.shape, lambda *_: zeros, pipeline_mode=pl.Buffered(1))


def of_layer(weights, layer):
    return pl.BlockSpec(
        (None, *weights.shape[1:]), lambda *_: (layer, 0, 0, 0), pipeline_mode=pl.Buffered(1)
    )


def params():
    return pltpu.CompilerParams(vmem_limit_bytes=VMEM_LIMIT, dimension_semantics=("arbitrary",))


def cost(images, layers):
    return pl.CostEstimate(
        flops=int(images * layers * 1.6e9), bytes_accessed=int(images * 4e6), transcendentals=int(images * 1e6)
    )


def live_step(k, where):
    return jnp.minimum(k, (where[0] - 1) // PAIR)


def by_step(shape):
    zeros = (0,) * len(shape)
    return pl.BlockSpec((1, *shape), lambda k, where: (live_step(k, where), *zeros))


def by_pair():
    return pl.BlockSpec((PAIR, PAD, D), lambda k, where: (live_step(k, where), 0, 0))


def by_image(micro, slots):
    def spec(image, core):
        def at(k, where):
            found = jnp.int32(0)
            for earlier in range(LIST // PAIR):
                entry = where[1 + PAIR * earlier + image]
                use = (earlier <= k) & (entry // (micro * slots) == core)
                found = jnp.where(use, entry % (micro * slots), found)
            return (found // slots, found % slots, 0, 0)

        return pl.BlockSpec((1, 1, TOK, D), at)

    return [spec(image, core) for image in range(PAIR) for core in range(2)]


def run_first(where, images, others, weights, perm, perm_t, bias):
    steps = LIST // PAIR
    outs = list(KEPT.values())
    return pl.pallas_call(
        first_kernel,
        grid_spec=pltpu.PrefetchScalarGridSpec(
            num_scalar_prefetch=1,
            grid=(steps,),
            in_specs=by_image(*images.shape[:2])
            + [of_layer(weights, 0)]
            + [whole(array) for array in (perm, perm_t, bias)],
            out_specs=[by_pair()] + [by_step(shape) for shape, _ in outs],
            scratch_shapes=scratch(LOCAL_F) + [pltpu.VMEM((BOTH, D), f32), pltpu.VMEM((16, D), f32)],
        ),
        out_shape=[IMAGES]
        + [jax.ShapeDtypeStruct((steps, *shape), dtype) for shape, dtype in outs],
        compiler_params=params(),
        cost_estimate=cost(LIST, 1),
        name="layer0_forward",
    )(where, images, others, images, others, weights, perm, perm_t, bias)


IMAGES = jax.ShapeDtypeStruct((LIST, PAD, D), bf16)
GRADS = jax.ShapeDtypeStruct((BLOCKS, GRAD_ROWS, D), bf16)
HALF = jax.ShapeDtypeStruct((BLOCKS // 2, GRAD_ROWS, D), bf16)


def run_second(where, rows, out_grad, others, weights, perm, perm_t, bias):
    return pl.pallas_call(
        second_kernel,
        grid_spec=pltpu.PrefetchScalarGridSpec(
            num_scalar_prefetch=1,
            grid=(LIST // PAIR,),
            in_specs=[by_pair()]
            + by_image(*out_grad.shape[:2])
            + [of_layer(weights, 1)]
            + [whole(array) for array in (perm, perm_t, bias)],
            out_specs=[by_pair(), by_pair(), by_pair(), whole(GRADS)],
            scratch_shapes=scratch({**KEPT, **LOCAL_F})
            + scratch(LOCAL_B)
            + [
                pltpu.VMEM((BOTH, D), f32),
                pltpu.VMEM((BOTH, D), f32),
                pltpu.VMEM((16, D), f32),
                pltpu.VMEM((128, 128), f32),
            ],
        ),
        out_shape=[IMAGES, IMAGES, IMAGES, GRADS],
        compiler_params=params(),
        cost_estimate=cost(LIST, 3),
        name="layer1_both",
    )(where, rows, out_grad, others, out_grad, others, weights, perm, perm_t, bias)


def run_third(where, images, others, grads, weights, perm, perm_t, kept):
    return pl.pallas_call(
        third_kernel,
        grid_spec=pltpu.PrefetchScalarGridSpec(
            num_scalar_prefetch=1,
            grid=(LIST // PAIR,),
            in_specs=by_image(*images.shape[:2])
            + [by_pair(), of_layer(weights, 0), whole(perm), whole(perm_t)]
            + [by_step(shape) for shape, _ in KEPT.values()],
            out_specs=[by_pair(), by_pair(), whole(HALF), whole(HALF)],
            scratch_shapes=scratch(LOCAL_B)
            + [
                pltpu.VMEM((BOTH, D), bf16),
                pltpu.VMEM((BOTH, D), f32),
                pltpu.VMEM((BOTH, D), f32),
                pltpu.VMEM((16, D), f32),
                pltpu.VMEM((128, 128), f32),
            ],
        ),
        out_shape=[IMAGES, IMAGES, HALF, HALF],
        compiler_params=params(),
        cost_estimate=cost(LIST, 2),
        name="layer0_backward",
    )(where, images, others, images, others, grads, weights, perm, perm_t, *kept)


def run_spread(flags, lists, micro, slots, dtype):
    def spec(slot, kind):
        def at(m, flags):
            i = m * slots + slot
            return (jnp.where(flags[i] == kind, flags[micro * slots + i], 0), 0, 0)

        return pl.BlockSpec((1, PAD, D), at)

    return pl.pallas_call(
        spread_kernel,
        grid_spec=pltpu.PrefetchScalarGridSpec(
            num_scalar_prefetch=1,
            grid=(micro,),
            in_specs=[spec(slot, kind) for slot in range(slots) for kind in range(4)],
            out_specs=pl.BlockSpec((1, TOK, slots, D), lambda m, flags: (m, 0, 0, 0)),
            scratch_shapes=[pltpu.VMEM((slots, PAD, D), bf16)],
        ),
        out_shape=jax.ShapeDtypeStruct((micro, TOK, slots, D), dtype),
        compiler_params=params(),
        name="spread_images",
    )(flags, *(list(lists) * slots))


def add_kernel(chip_ref, keep_ref, got_ref, *out_refs):
    chips = len(out_refs)
    for d, out_ref in enumerate(out_refs):
        at = lax.rem(chip_ref[0] + d, chips)
        out_ref[...] = (keep_ref[at].astype(f32) + got_ref[at].astype(f32)).astype(bf16)


def run_add(chip, keep, got):
    chips = keep.shape[0]
    one = jax.ShapeDtypeStruct((GRAD_ROWS, D), bf16)
    in_vmem = pl.BlockSpec(memory_space=pltpu.VMEM)
    return pl.pallas_call(
        add_kernel,
        grid_spec=pltpu.PrefetchScalarGridSpec(
            num_scalar_prefetch=1,
            grid=(),
            in_specs=[in_vmem] * 2,
            out_specs=[in_vmem] * chips,
        ),
        out_shape=[one] * chips,
        compiler_params=pltpu.CompilerParams(vmem_limit_bytes=VMEM_LIMIT),
        name="add_cores",
    )(chip.reshape(1).astype(jnp.int32), keep, got)


def parts_kernel(section_ref, first_ref, *refs):
    own_ref, send_ref = refs[-2:]
    total = refs[0][...].astype(f32)
    for ref in refs[1:-2]:
        total = total + ref[...].astype(f32)
    total = total.astype(bf16)
    for section in range(2):

        @pl.when(section_ref[0] == section)
        def _():
            own_ref[...] = first_ref[...] if section else total
            send_ref[...] = total if section else first_ref[...]


def run_parts(section, sums1, parts):
    one = jax.ShapeDtypeStruct(sums1.shape, bf16)
    spec = pl.BlockSpec((sums1.shape[0] // 2, D), lambda i, section: (i, 0))
    return pl.pallas_call(
        parts_kernel,
        grid_spec=pltpu.PrefetchScalarGridSpec(
            num_scalar_prefetch=1,
            grid=(2,),
            in_specs=[spec] * (1 + len(parts)),
            out_specs=[spec] * 2,
        ),
        out_shape=[one] * 2,
        compiler_params=params(),
        name="add_chips",
    )(section.reshape(1).astype(jnp.int32), sums1, *parts)


def final_kernel(place_ref, *refs):
    own_ref, got_ref, *out_refs, total_ref = refs
    gains_ref, vectors_ref, qkv_ref, proj_ref, hidden_ref, bias_ref, out_ref, table_ref = out_refs
    total_ref[...] = own_ref[...].astype(f32) + got_ref[...].astype(f32)
    index = place_ref[0]
    rows, width = qkv_ref.shape[0], out_ref.shape[0]
    for at in range(3):
        qkv_ref[:, at * D : (at + 1) * D] = total_ref[at * rows : (at + 1) * rows, :]
    proj_ref[...] = total_ref[3 * rows : 4 * rows, :]
    for at in range(CH):
        hidden_ref[:, at * D : (at + 1) * D] = total_ref[(4 + at) * rows : (5 + at) * rows, :]
    if width == FF // BLOCKS:
        for at in range(D // width):
            lanes = slice(at * width, (at + 1) * width)
            out_ref[:, lanes] = total_ref[8 * rows : 8 * rows + width, lanes].T
    else:
        out_ref[...] = total_ref[8 * rows : 8 * rows + width, :]
    small = total_ref[8 * rows + width : 8 * rows + width + 16, :]
    own = pltpu.roll(small, D - index * rows, 1)
    gains_ref[...] = own[0:2, :rows]
    for at in range(6):
        vectors_ref[at] = own[2 + at : 3 + at, :rows]
    row = lax.broadcasted_iota(jnp.int32, (16, D), 0)
    mine = jnp.where(row == 8 + index * width // D, small, 0.0)
    mine = jnp.sum(mine, axis=0, keepdims=True)
    mine = pltpu.roll(jnp.broadcast_to(mine, (8, D)), D - lax.rem(index * width, D), 1)
    bias_ref[...] = mine[0:1, :width]
    side = 2 * WIN - 1
    goal = lax.broadcasted_iota(jnp.int32, (TABLE, 256), 0)
    lane = lax.broadcasted_iota(jnp.int32, (TABLE, 256), 1)
    pick = (lane == 16 * (goal // side) + lax.rem(goal, side)).astype(f32)
    table = total_ref[8 * rows + width + 16 : 8 * rows + width + 32, 0:256]
    table_ref[...] = lax.dot_general(
        table,
        pick,
        (((1,), (1,)), ((), ())),
        precision=lax.Precision.HIGHEST,
        preferred_element_type=f32,
    )


def run_final(index, own, got, shards):
    rows, width = D // shards, FF // shards
    shapes = [
        (2, rows), (6, 1, rows), (rows, 3 * D), (rows, D), (rows, FF), (1, width), (width, D), (HEADS, TABLE)
    ]
    outs = pl.pallas_call(
        final_kernel,
        grid_spec=pltpu.PrefetchScalarGridSpec(
            num_scalar_prefetch=1,
            grid=(),
            in_specs=[pl.BlockSpec(memory_space=pltpu.VMEM)] * 2,
            out_specs=[pl.BlockSpec(memory_space=pltpu.VMEM)] * 8,
            scratch_shapes=[pltpu.VMEM(own.shape, f32)],
        ),
        out_shape=[jax.ShapeDtypeStruct(shape, f32) for shape in shapes],
        name="final_sums",
    )(index.reshape(1).astype(jnp.int32), own, got)
    outs = list(outs)
    outs[1] = outs[1].reshape(6, rows)
    outs[5] = outs[5].reshape(width)
    outs[7] = outs[7].T
    return outs


def pack_kernel(qkv_ref, proj_ref, hidden_ref, out_ref, small_ref, packed_ref):
    rows = qkv_ref.shape[0]
    for at in range(3):
        packed_ref[at * rows : (at + 1) * rows, :] = qkv_ref[:, at * D : (at + 1) * D]
    packed_ref[3 * rows : 4 * rows, :] = proj_ref[...]
    for at in range(CH):
        packed_ref[(4 + at) * rows : (5 + at) * rows, :] = hidden_ref[:, at * D : (at + 1) * D]
    width = out_ref.shape[0]
    packed_ref[8 * rows : 8 * rows + width, :] = out_ref[...]
    packed_ref[8 * rows + width : 8 * rows + width + 16, :] = small_ref[...]


def pack_weights(norm_gains, vectors, qkv, proj, hidden, hidden_bias, out, index, shards):
    small = jnp.concatenate([norm_gains[0], vectors[0]], axis=0)
    mine = jnp.arange(shards)[None, :, None] == index
    small = jnp.where(mine, small[:, None, :], jnp.zeros((), bf16)).reshape(8, D)
    bias = jnp.where(mine[0], hidden_bias, jnp.zeros((), bf16)).reshape(CH, D)
    small = jnp.concatenate([small, bias, jnp.zeros((4, D), bf16)], axis=0)
    rows = 8 * qkv.shape[1] + out.shape[1] + 16
    return pl.pallas_call(
        pack_kernel, out_shape=jax.ShapeDtypeStruct((rows, D), bf16), name="pack_weights"
    )(qkv[0], proj[0], hidden[0], out[0], small)


def regroup(array, rows_from, rows_to, goal):
    pieces, at = [], 0
    for rows, new_rows in zip(rows_from, rows_to):
        pieces.append(array[:, at : at + rows].reshape(goal, new_rows, D))
        at += rows
    return pieces


def merge_shards(gathered, shards):
    rows = D // shards
    parts = [rows] * 8 + [FF // shards]
    goals = [ROWS] * 8 + [FF // BLOCKS]
    pieces = regroup(gathered[:, : sum(parts)], parts, goals, BLOCKS)
    small = jnp.sum(gathered[:, sum(parts) :].astype(f32), axis=0).astype(bf16)
    small = jnp.where(jnp.arange(BLOCKS)[:, None, None] == 0, small[None], jnp.zeros((), bf16))
    return jnp.concatenate(pieces + [small], axis=1)


def shift(array, by):
    chips = lax.axis_size("chip")
    return lax.ppermute(array, "chip", [(i, (i + by) % chips) for i in range(chips)])


def split_shards(packed, shards):
    if shards == BLOCKS:
        return packed
    rows, width = D // shards, FF // BLOCKS
    parts = [ROWS] * 8 + [width]
    goals = [rows] * 8 + [FF // shards]
    turned = packed[:, OUT_AT:SMALL_AT].reshape(BLOCKS, width, D // width, width)
    turned = turned.transpose(0, 3, 2, 1).reshape(BLOCKS, width, D)
    blocks = jnp.concatenate([packed[:, :OUT_AT], turned], axis=1)
    pieces = regroup(blocks, parts, goals, shards)
    small = jnp.broadcast_to(packed[:1, SMALL_AT:], (shards, GRAD_ROWS - SMALL_AT, D))
    return jnp.concatenate(pieces + [small], axis=1)


def on_device(
    images,
    live_counts,
    norm_gains,
    vectors,
    qkv_weight,
    proj_weight,
    hidden_weight,
    hidden_bias,
    out_weight,
    bias_table,
    out_grad,
):
    micro, slots = images.shape[:2]
    every = micro * slots
    section = lax.axis_index("section")
    core = lax.axis_index("core")
    shards = lax.axis_size("chip") * lax.axis_size("core")
    index = lax.axis_index("chip") * lax.axis_size("core") + core
    is_first = section == 0

    packed = pack_weights(
        norm_gains, vectors, qkv_weight, proj_weight, hidden_weight, hidden_bias, out_weight, index, shards
    )
    gathered = lax.all_gather(packed, ("section", *SHARDED)).reshape(2, shards, *packed.shape)
    if shards == BLOCKS:
        weights = gathered
    else:
        weights = jnp.stack([merge_shards(gathered[layer], shards) for layer in range(2)])

    other_table = lax.ppermute(bias_table[0], "section", SWAP)
    bias0 = bias_arrays(jnp.where(is_first, bias_table[0], other_table), False)
    bias1 = bias_arrays(jnp.where(is_first, other_table, bias_table[0]), True)
    perms = permutations()
    perm0, perm1 = (jnp.asarray(mat, bf16) for mat in perms)
    perm0_t, perm1_t = (jnp.asarray(mat.T, bf16) for mat in perms)

    counts = live_counts[:, 0]
    other_counts = lax.ppermute(counts, "core", SWAP)
    counts = jnp.stack([jnp.where(core == 0, counts, other_counts), jnp.where(core == 0, other_counts, counts)])
    live = (jnp.arange(slots)[None, None, :] < counts[:, :, None]).reshape(-1)
    place = jnp.cumsum(live.astype(jnp.int32)) - 1
    total = jnp.sum(live.astype(jnp.int32))
    rank = 2 * core + section
    chip = lax.axis_index("chip")
    split_core = core if shards == BLOCKS else jnp.int32(0)
    count = (total - rank + 3) // 4
    wanted = jnp.minimum(jnp.arange(LIST), count - 1) * 4 + rank
    hits = live[None, :] & (place[None, :] == wanted[:, None])
    entry = jnp.arange(2 * every)
    entry = jnp.where(entry // every == core, entry % every, every + entry % every)
    mine = jnp.sum(jnp.where(hits, entry[None, :], 0), axis=1)
    where = jnp.concatenate([count[None], mine, jnp.full((1,), every), split_core[None], chip[None], section[None]]).astype(jnp.int32)
    live = lax.dynamic_slice(live, (core * every,), (every,))
    place = lax.dynamic_slice(place, (core * every,), (every,))
    kind = 2 * (place % 4 // 2 != core).astype(jnp.int32) + (place % 2 != section).astype(jnp.int32)
    flags = jnp.concatenate([jnp.where(live, kind, 4), jnp.maximum(place, 0) // 4]).astype(jnp.int32)
    other_images = lax.ppermute(images, "core", SWAP)
    other_out_grad = lax.ppermute(out_grad, "core", SWAP)

    def assemble(own, got, dtype):
        others = [lax.ppermute(rows, "core", SWAP) for rows in (own, got)]
        return run_spread(flags, [own, got, *others], micro, slots, dtype)

    rows0, *kept = run_first(where, images, other_images, weights, perm0, perm0_t, bias0)
    own_rows, sent_rows, grads1, packed1 = run_second(
        where, rows0, out_grad, other_out_grad, weights, perm1, perm1_t, bias1
    )
    got_rows = lax.ppermute(sent_rows, "section", SWAP)
    sums1 = lax.psum_scatter(split_shards(packed1, shards), SHARDED, scatter_dimension=0)
    own_grads, sent_grads, keep0, send0 = run_third(
        where, images, other_images, grads1, weights, perm0, perm0_t, kept
    )
    own_grads, sent_grads, keep0, send0, got_rows = lax.optimization_barrier(
        (own_grads, sent_grads, keep0, send0, got_rows)
    )
    if shards == BLOCKS:
        got0 = lax.ppermute(send0, "core", SWAP)
        blocks = run_add(chip, keep0, got0)
        blocks, sent_grads, own_grads, own_rows = lax.optimization_barrier(
            (blocks, sent_grads, own_grads, own_rows)
        )
        parts = [blocks[0]] + [shift(blocks[d], d) for d in range(1, len(blocks))]
    else:
        packed0 = jnp.stack([keep0, send0], axis=1).reshape(GRADS.shape)
        parts = [lax.psum_scatter(split_shards(packed0, shards), SHARDED, scatter_dimension=0)]
    got_grads = lax.ppermute(sent_grads, "section", SWAP)
    layer_out = assemble(own_rows, got_rows, bf16)
    parts, sums1, layer_out = lax.optimization_barrier((parts, sums1, layer_out))
    own_sums, sent_sums = run_parts(section, sums1, parts)
    got_sums = lax.ppermute(sent_sums, "section", SWAP)
    own_grads, own_sums = lax.optimization_barrier((own_grads, own_sums))
    input_out = assemble(own_grads, got_grads, f32)
    got_sums, input_out = lax.optimization_barrier((got_sums, input_out))
    finals = run_final(index, own_sums, got_sums, shards)
    return (
        layer_out.transpose(0, 2, 1, 3)[None],
        input_out.transpose(0, 2, 1, 3)[None],
        *[array[None] for array in finals],
    )


def solution(mesh):
    shape = (mesh.shape["section"], mesh.shape["fsdp"] // 2, 2)
    mesh = jax.sharding.Mesh(mesh.devices.reshape(shape), ("section", *SHARDED))
    in_specs = (
        P(None, SHARDED, None, None),
        P(None, SHARDED),
        P("section", None, SHARDED),
        P("section", None, SHARDED),
        P("section", SHARDED, None),
        P("section", SHARDED, None),
        P("section", SHARDED, None),
        P("section", SHARDED),
        P("section", SHARDED, None),
        P("section", None, None),
        P(None, SHARDED, None, None),
    )
    out_specs = (
        P("section", None, SHARDED, None, None),
        P("section", None, SHARDED, None, None),
        P("section", None, SHARDED),
        P("section", None, SHARDED),
        P("section", SHARDED, None),
        P("section", SHARDED, None),
        P("section", SHARDED, None),
        P("section", SHARDED),
        P("section", SHARDED, None),
        P("section", None, None),
    )
    return jax.shard_map(
        on_device, mesh=mesh, in_specs=in_specs, out_specs=out_specs, check_vma=False
    )
```

time: 2180 us -> 414 us (0.19)
  local copies, waits for them, and re-layouts: 897 us -> 22.4 us
  matrix products: 558 us -> 2.08 us
  other arithmetic: 213 us -> 4.76 us
  waiting for transfers between devices: 304 us -> 102 us
  Pallas kernels: 0 us -> 188 us
  blocking collectives: 139 us -> 0 us
  starting transfers between devices: 23.5 us -> 77.9 us
    dot_general x112 -> x2, matrix products: 558 us -> 2.08 us  [bias_arrays(): flat = jnp.dot(pick.astype(f32), table, precision=lax.Precision.HIGHEST)]
    reduce_scatter x4 -> x1, waiting for transfers between devices: 246 us -> 0.01 us  [on_device(): lax.psum_scatter(split_shards(packed1, shards), SHARDED, scatter_dimensio...]
    convert_element_type x55 -> x1, local copies, waits for them, and re-layouts: 225 us -> 0.08 us  [on_device(): total = jnp.sum(live.astype(jnp.int32))]
    unnamed x794 -> x35, local copies, waits for them, and re-layouts: 217 us -> 10.1 us
    reshape x44 -> x2, local copies, waits for them, and re-layouts: 201 us -> 1.26 us  [the longest x1 1.05 us: bias_arrays(): return bias.reshape(bias.shape[0], GROUPS, WTOK, GROUP * WTOK)]
    pallas_call x0 -> x9, Pallas kernels: none -> 188 us  [the longest x1 78 us: run_second(): pl.pallas_call(second_kernel, grid_spec=pltpu.PrefetchScalarGridSpec(num_...]
    slice x80 -> x0, local copies, waits for them, and re-layouts: 116 us -> none  [the longest x5 34.4 us: layer_forward(): values_in = pieces[:, :, 2]]
    reduce_sum x67 -> x2, other arithmetic: 87.4 us -> 0.89 us  [the longest x1 0.7 us: on_device(): total = jnp.sum(live.astype(jnp.int32))]
  transfers between devices with their start and end apart: 18 -> 21, of which waited for: 9 -> 7; matrix products, arithmetic and copies ran while one was open for 15% -> 6% of each run, Pallas kernels for 0% -> 18%
where the time goes in v1:
time: 414 us; the launch traced here: 412 us
  Pallas kernels  188 us (45%)
  waiting for transfers between devices  102 us (25%)
  starting transfers between devices  77.9 us (19%)
  local copies, waits for them, and re-layouts  22.4 us (5%)
  between operations  15.2 us (4%)
  other arithmetic  4.76 us (1%)
    pallas_call x1, Pallas kernels, run_second(): pl.pallas_call(second_kernel, grid_spec=pltpu.PrefetchScalarGridSpec(num_...  78 us
    all_gather x1, waiting for transfers between devices, on_device(): lax.all_gather(packed, ('section', *SHARDED))  73.4 us
    ppermute x7, starting transfers between devices, shift(): lax.ppermute(array, 'chip', [(i, (i + by) % chips) for i in range(chips)])  69.7 us
    pallas_call x1, Pallas kernels, run_third(): pl.pallas_call(third_kernel, grid_spec=pltpu.PrefetchScalarGridSpec(num_s...  46.3 us
    pallas_call x1, Pallas kernels, run_first(): pl.pallas_call(first_kernel, grid_spec=pltpu.PrefetchScalarGridSpec(num_s...  32.9 us
    ppermute x7, waiting for transfers between devices, shift(): lax.ppermute(array, 'chip', [(i, (i + by) % chips) for i in range(chips)])  19.8 us
    pallas_call x2, Pallas kernels, run_spread(): pl.pallas_call(spread_kernel, grid_spec=pltpu.PrefetchScalarGridSpec(num_...  18.3 us
    unnamed x35, local copies, waits for them, and re-layouts  10.1 us
  transfers between devices with their start and end apart: 21, of which 7 were waited for; matrix products, arithmetic and copies ran while one was open for 6% of the time, Pallas kernels for 18%

profile of v1, /device:TPU:0, one launch (start us, length us, event | category | flops | bytes accessed | tf_op | source)
XLA Modules:
  0.0 412.3 jit_solution(11613146810923555285)
XLA Ops:
  7.3 0.6 copy-done
  7.8 0.1 broadcast_in_dim.146
  7.9 0.1 broadcast_in_dim.147
  8.0 0.1 broadcast_bitcast_fusion
  8.1 0.7 pad_maximum_fusion.1
  8.8 0.1 broadcast_in_dim.150
  8.9 0.6 pad_maximum_fusion.small_ref
  9.6 1.8 pack_weights.1
  11.4 0.5 collective-permute-start.1
  12.0 0.1 collective-permute-start.3
  12.0 0.4 collective-permute-start
  12.5 2.6 collective-permute-start.2
  15.0 4.5 %copy.78.x0.x2 = bf16[4,4,196,512]{3,2,1,0:T(8,128)(2,1)} copy(bf16[4,4,196,512]{3,1,2,0:T(4,128)(2,1)} %param.20) | data formatting | bytes 6422528 | tf_op args[0]
  19.6 2.3 copy.74.e0.e2
  21.9 0.1 add.105
  22.0 0.3 add.106
  22.4 0.7 convert_reduce_fusion
  23.8 0.1 iota_compare_fusion.3
  23.8 0.1 lt.57
  23.9 0.1 reshape.166
  24.1 0.1 broadcast_add_fusion
  24.2 0.2 select_reduce_fusion
  24.4 0.6 concatenate.12.where_ref
  25.0 1.0 convolution_multiply_fusion
  26.0 0.2 mul.43
  26.3 0.4 fusion.3
  26.7 1.0 reshape.160.bias_ref
  27.7 1.0 fusion
  28.8 0.2 reshape.161
  29.0 0.3 copy.73
  29.3 0.3 add.103
  29.7 1.2 multiply_select_fusion.bias_ref
  30.9 4.2 %copy.79.x1.x3 = bf16[4,4,196,512]{3,2,1,0:T(8,128)(2,1)} copy(bf16[4,4,196,512]{3,1,2,0:T(4,128)(2,1)} %collective-permute-done.1) | data formatting | bytes 6422528 | tf_op jit(solution)/shard_map/ppermute | solution.py:994
  35.1 4.2 %copy.75.e1.e3 = bf16[4,4,196,512]{3,2,1,0:T(8,128)(2,1)} copy(bf16[4,4,196,512]{3,1,2,0:T(4,128)(2,1)} %collective-permute-done.3) | data formatting | bytes 6422528 | tf_op jit(solution)/shard_map/ppermute | solution.py:995
  39.3 73.4 %all-gather.3.cloned.1.call-done = bf16[12800,512]{1,0:T(8,128)(2,1)} async-done(((bf16[400,512]{1,0:T(8,128)(2,1)}), bf16[12800,512]{1,0:T(8,128)(2,1)}) %all-gather.3.cloned.1.call-update) | async-done | bytes 13107216 | tf_op jit(solution)/shard_map/all_gather | solution.py:961
  112.7 32.9 %layer0_forward.1 = (bf16[8,208,512]{2,1,0:T(8,128)(2,1)}, bf16[4,512,512]{2,1,0:T(8,128)(2,1)}, bf16[4,512,512]{2,1,0:T(8,128)(2,1)}, bf16[4,512,512]{2,1,0:T(8...) custom-call(s32[13]{0:T(128)} %concatenate.12.where_ref, ...), custom_call_target="tpu_custom_call" | custom-call | flops 12800000000 | bytes 32000000 | tf_op jit(solution)/shard_map/layer0_forward/pallas_call | solution.py:655
  145.6 78.0 %layer1_both.1 = (bf16[8,208,512]{2,1,0:T(8,128)(2,1)}, bf16[8,208,512]{2,1,0:T(8,128)(2,1)}, bf16[8,208,512]{2,1,0:T(8,128)(2,1)}, bf16[16,416,512]{2,1,0:T(8,128)(2,1)}) custom-call(s32[13]{0:T(128)} %concatenate.12.where_ref, bf16[8,208,512]{2,1,0:T(8,128)(2,1)} %get-tuple-element.75.x_ref, bf16[4,4,196,512]{3,2,1,0:T(8,128)(2,1)} %copy.74.e0.e2, ...), custom_call_target="tpu_custom_call" | custom-call | flops 38400000000 | bytes 32000000 | tf_op jit(solution)/shard_map/layer1_both/pallas_call | solution.py:680
  223.6 1.4 copy-done.13
  225.0 1.4 collective-permute-start.4
  226.4 46.3 %layer0_backward.1 = (bf16[8,208,512]{2,1,0:T(8,128)(2,1)}, bf16[8,208,512]{2,1,0:T(8,128)(2,1)}, bf16[8,416,512]{2,1,0:T(8,128)(2,1)}, bf16[8,416,512]{2,1,0:T(8,128)(2,1)}) custom-call(s32[13]{0:T(128)} %concatenate.12.where_ref, bf16[4,4,196,512]{3,2,1,0:T(8,128)(2,1)} %copy.78.x0.x2, bf16[4,4,196,512]{3,2,1,0:T(8,128)(2,1)} %copy.79.x1.x3, ...), custom_call_target="tpu_custom_call" | custom-call | flops 25600000000 | bytes 32000000 | tf_op jit(solution)/shard_map/layer0_backward/pallas_call | solution.py:707
  272.8 0.5 collective-permute-start.14
  273.3 5.9 %collective-permute-done.5.got_ref = bf16[8,416,512]{2,1,0:T(8,128)(2,1)} collective-permute-done((bf16[8,416,512]{2,1,0:T(8,128)(2,1)}, bf16[8,416,512]{2,1,0:T(8,128)(2,1)}, u32[]{:S(2)}, u32[]{:S(2)}) %collective-permute-start.5) | collective-permute-done | bytes 3407904 | tf_op jit(solution)/shard_map/ppermute | solution.py:1014
  279.1 5.5 %add_cores.1 = (bf16[416,512]{1,0:T(8,128)(2,1)}, bf16[416,512]{1,0:T(8,128)(2,1)}, bf16[416,512]{1,0:T(8,128)(2,1)}, bf16[416,512]{1,0:T(8,128)(2,1)}, bf16[416...) custom-call(s32[1]{0:T(128)} %bitcast.chip_ref, ...), custom_call_target="tpu_custom_call" | custom-call | tf_op jit(solution)/shard_map/add_cores/pallas_call | solution.py:766
  284.6 0.2 collective-permute-start.13
  284.8 0.7 collective-permute-start.16
  285.5 1.5 collective-permute-start.6
  287.0 0.6 collective-permute-start.7
  287.6 1.3 collective-permute-start.8
  288.8 12.7 %collective-permute-done.6.refs_1_ = bf16[416,512]{1,0:T(8,128)(2,1)S(1)} collective-permute-done((bf16[416,512]{1,0:T(8,128)(2,1)}, bf16[416,512]{1,0:T(8,128)(2,1)S(1)}, u32[]{:S(2)}, u32[]{:S(2)}) %collective-permute-start.6) | collective-permute-done | bytes 426016 | tf_op jit(solution)/shard_map/ppermute | solution.py:920
  301.6 2.1 collective-permute-done.7.refs_2_
  303.6 56.3 %collective-permute-start.10 = (bf16[416,512]{1,0:T(8,128)(2,1)}, bf16[416,512]{1,0:T(8,128)(2,1)}, u32[]{:S(2)}, u32[]{:S(2)}) collective-permute-start(bf16[416,512]{1,0:T(8,128)(2,1)} %get-tuple-element.108), channel_id=1, source_target_pairs={{0,10},{2,12},{4,14},{6,0},{8,2},{10,4},{12,6},{14,8},{1,11},{3,13... | collective-permute-start | bytes 1277960 | tf_op jit(solution)/shard_map/ppermute | solution.py:920
  360.0 10.0 %collective-permute-start.11 = (bf16[416,512]{1,0:T(8,128)(2,1)}, bf16[416,512]{1,0:T(8,128)(2,1)}, u32[]{:S(2)}, u32[]{:S(2)}) collective-permute-start(bf16[416,512]{1,0:T(8,128)(2,1)} %get-tuple-element.109), channel_id=1, source_target_pairs={{0,12},{2,14},{4,0},{6,2},{8,4},{10,6},{12,8},{14,10},{1,13},{3,15... | collective-permute-start | bytes 1277960 | tf_op jit(solution)/shard_map/ppermute | solution.py:920
  370.0 1.2 copy-done.5
  371.2 0.1 dynamic-slice_reduce_fusion
  371.3 0.1 dynamic-slice_select_fusion
  371.4 0.6 pad_add_fusion.1.flags_ref
  372.0 10.0 %spread_images.2 = bf16[4,196,4,512]{3,2,1,0:T(4,128)(2,1)} custom-call(s32[32]{0:T(128)} %pad_add_fusion.1.flags_ref, bf16[8,208,512]{2,1,0:T(8,128)(2,1)} %get-tuple-element.112.refs_0_.refs_4_.refs_8_.refs_12_, bf16[8,208,512]{2,1,0:T(8,128)(2,1)} %collective-permute-done.4.refs_1_.refs_5_.refs_9_.refs_13_, bf16[8,208,512]{2,1,0:T(8,128)(2,1)} %copy-done.5, ...), custom_call_target="tpu_custom_call" | custom-call | tf_op jit(solution)/shard_map/spread_images/pallas_call | solution.py:740
  382.2 5.0 %collective-permute-done.12.refs_7_ = bf16[416,512]{1,0:T(8,128)(2,1)} collective-permute-done((bf16[416,512]{1,0:T(8,128)(2,1)}, bf16[416,512]{1,0:T(8,128)(2,1)}, u32[]{:S(2)}, u32[]{:S(2)}) %collective-permute-start.12) | collective-permute-done | bytes 426016 | tf_op jit(solution)/shard_map/ppermute | solution.py:920
  387.1 3.3 add_chips.1
  390.5 1.6 collective-permute-start.15
  392.2 2.1 collective-permute-done.17.refs_2_.refs_6_.refs_10_.refs_14_
  394.2 8.2 %spread_images.3 = f32[4,196,4,512]{3,2,1,0:T(4,128)} custom-call(s32[32]{0:T(128)} %pad_add_fusion.1.flags_ref, bf16[8,208,512]{2,1,0:T(8,128)(2,1)} %get-tuple-element.127.refs_0_.refs_4_.refs_8_.refs_12_, bf16[8,208,512]{2,1,0:T(8,128)(2,1)} %copy-done.4, bf16[8,208,512]{2,1,0:T(8,128)(2,1)} %collective-permute-done.17.refs_2_.refs_6_.refs_10_.refs_14_, ...), custom_call_target="tpu_custom_call" | custom-call | tf_op jit(solution)/shard_map/spread_images/pallas_call | solution.py:740
  402.5 0.6 collective-permute-done.15.refs_1_
  403.1 2.2 final_sums.1
  (64 shorter events, 0.6 us)
Async XLA Ops:
  7.2 0.7 copy-start
  7.2 105.5 %all-gather.3.cloned.1.call-start = ((), (), s32[]{:S(2)}) async-start(), calls=%async_computation.2 | async-start | bytes 13516800 | tf_op jit(solution)/shard_map/all_gather | solution.py:961
  11.4 375.7 %reduce-scatter.2.cloned.1.call-start = ((), (), s32[]{:S(2)}) async-start(), calls=%async_computation.1 | async-start | bytes 7241728 | tf_op jit(solution)/shard_map/reduce_scatter | solution.py:1006
  11.4 19.4 %collective-permute-start.1 = (bf16[4,4,196,512]{3,1,2,0:T(4,128)(2,1)}, bf16[4,4,196,512]{3,1,2,0:T(4,128)(2,1)}, u32[]{:S(2)}, u32[]{:S(2)}) collective-permute-start(bf16[4,4,196,512]{3,1,2,0:T(4,128)(2,1)} %param.20), channel_id=1, source_target_pairs={{0,1},{1,0},{2,3},{3,2},{4,5},{5,4},{6,7},{7,6},{8,9},{9,8},{10,11... | collective-permute-start | bytes 9633800 | tf_op jit(solution)/shard_map/ppermute | solution.py:994
  12.0 23.1 %collective-permute-start.3 = (bf16[4,4,196,512]{3,1,2,0:T(4,128)(2,1)}, bf16[4,4,196,512]{3,1,2,0:T(4,128)(2,1)}, u32[]{:S(2)}, u32[]{:S(2)}) collective-permute-start(bf16[4,4,196,512]{3,1,2,0:T(4,128)(2,1)} %param.30), channel_id=1, source_target_pairs={{0,1},{1,0},{2,3},{3,2},{4,5},{5,4},{6,7},{7,6},{8,9},{9,8},{10,11... | collective-permute-start | bytes 9633800 | tf_op jit(solution)/shard_map/ppermute | solution.py:995
  12.0 10.3 %collective-permute-start = (s32[4]{0:T(128)}, s32[4]{0:T(128)S(1)}, u32[]{:S(2)}, u32[]{:S(2)}) collective-permute-start(s32[4]{0:T(128)} %bitcast.69), channel_id=1, source_target_pairs={{0,1},{1,0},{2,3},{3,2},{4,5},{5,4},{6,7},{7,6},{8,9},{9,8},{10,11... | collective-permute-start | bytes 56 | tf_op jit(solution)/shard_map/ppermute | solution.py:975
  12.5 12.5 %collective-permute-start.2 = (f32[169,16]{0,1:T(8,128)}, f32[169,16]{0,1:T(8,128)S(1)}, u32[]{:S(2)}, u32[]{:S(2)}) collective-permute-start(f32[169,16]{0,1:T(8,128)} %bitcast.77), channel_id=1, source_target_pairs={{0,16},{16,0},{1,17},{17,1},{2,18},{18,2},{3,19},{19,3},{4,20},{20... | collective-permute-start | bytes 32456 | tf_op jit(solution)/shard_map/ppermute | solution.py:967
  15.0 4.5 %copy-start.6 = (bf16[4,4,196,512]{3,1,2,0:T(4,128)(2,1)S(1)}, bf16[4,4,196,512]{3,1,2,0:T(4,128)(2,1)}, u32[]{:S(2)}) copy-start(bf16[4,4,196,512]{3,1,2,0:T(4,128)(2,1)} %param.30) | copy-start | bytes 9633796
  19.5 2.3 copy-start.10
  19.5 2.8 copy-start.12
  19.5 5.4 %copy-start.14 = (f32[1,169,16]{1,2,0:T(8,128)S(1)}, f32[1,169,16]{1,2,0:T(8,128)}, u32[]{:S(2)}) copy-start(f32[1,169,16]{1,2,0:T(8,128)} %param.29) | copy-start | bytes 32452
  19.5 5.4 %copy-start.15 = (s32[4096]{0:T(1024)S(1)}, s32[4096]{0:T(1024)}, u32[]{:S(2)}) copy-start(s32[4096]{0:T(1024)} %constant.158) | copy-start | bytes 49156
  21.9 4.4 %copy-start.11 = (pred[64]{0:T(512)(128)(4,1)S(1)}, pred[64]{0:T(512)(128)(4,1)}, u32[]{:S(2)}) copy-start(pred[64]{0:T(512)(128)(4,1)} %constant.141.clone) | copy-start | bytes 196
  223.6 1.5 copy-start.13
  225.0 47.7 %collective-permute-start.4 = (bf16[8,208,512]{2,1,0:T(8,128)(2,1)S(1)}, bf16[8,208,512]{2,1,0:T(8,128)(2,1)}, u32[]{:S(2)}, u32[]{:S(2)}) collective-permute-start(bf16[8,208,512]{2,1,0:T(8,128)(2,1)S(1)} %copy-done.13), channel_id=1, source_target_pairs={{0,16},{16,0},{1,17},{17,1},{2,18},{18,2},{3,19},{19,3},{4,20},{20... | collective-permute-start | bytes 5111816 | tf_op jit(solution)/shard_map/ppermute | solution.py:1005
  272.7 11.9 %copy-start.3 = (bf16[8,208,512]{2,1,0:T(8,128)(2,1)S(1)}, bf16[8,208,512]{2,1,0:T(8,128)(2,1)}, u32[]{:S(2)}) copy-start(bf16[8,208,512]{2,1,0:T(8,128)(2,1)} %get-tuple-element.112.refs_0_.refs_4_.refs_8_.refs_12_) | copy-start | bytes 5111812
  272.7 6.4 %collective-permute-start.5 = (bf16[8,416,512]{2,1,0:T(8,128)(2,1)}, bf16[8,416,512]{2,1,0:T(8,128)(2,1)}, u32[]{:S(2)}, u32[]{:S(2)}) collective-permute-start(bf16[8,416,512]{2,1,0:T(8,128)(2,1)} %get-tuple-element.91), channel_id=1, source_target_pairs={{0,1},{1,0},{2,3},{3,2},{4,5},{5,4},{6,7},{7,6},{8,9},{9,8},{10,11... | collective-permute-start | bytes 10223624 | tf_op jit(solution)/shard_map/ppermute | solution.py:1014
  272.8 14.8 %collective-permute-start.14 = (bf16[8,208,512]{2,1,0:T(8,128)(2,1)}, bf16[8,208,512]{2,1,0:T(8,128)(2,1)}, u32[]{:S(2)}, u32[]{:S(2)}) collective-permute-start(bf16[8,208,512]{2,1,0:T(8,128)(2,1)} %collective-permute-done.4.refs_1_.refs_5_.refs_9_.refs_13_), channel_id=1, source_target_pairs={{0,1},{1,0},{2,3},{3,2},{4,5},{5,4},{6,7},{7,6},{8,9},{9,8},{10,11... | collective-permute-start | bytes 5111816 | tf_op jit(solution)/shard_map/ppermute | solution.py:998
  284.6 85.3 %collective-permute-start.13 = (bf16[8,208,512]{2,1,0:T(8,128)(2,1)S(1)}, bf16[8,208,512]{2,1,0:T(8,128)(2,1)S(1)}, u32[]{:S(2)}, u32[]{:S(2)}) collective-permute-start(bf16[8,208,512]{2,1,0:T(8,128)(2,1)S(1)} %copy-done.3), channel_id=1, source_target_pairs={{0,1},{1,0},{2,3},{3,2},{4,5},{5,4},{6,7},{7,6},{8,9},{9,8},{10,11... | collective-permute-start | bytes 5111816 | tf_op jit(solution)/shard_map/ppermute | solution.py:998
  284.8 97.2 %collective-permute-start.16 = (bf16[8,208,512]{2,1,0:T(8,128)(2,1)}, bf16[8,208,512]{2,1,0:T(8,128)(2,1)S(1)}, u32[]{:S(2)}, u32[]{:S(2)}) collective-permute-start(bf16[8,208,512]{2,1,0:T(8,128)(2,1)} %get-tuple-element.128), channel_id=1, source_target_pairs={{0,16},{16,0},{1,17},{17,1},{2,18},{18,2},{3,19},{19,3},{4,20},{20... | collective-permute-start | bytes 5111816 | tf_op jit(solution)/shard_map/ppermute | solution.py:1023
  285.5 16.1 %collective-permute-start.6 = (bf16[416,512]{1,0:T(8,128)(2,1)}, bf16[416,512]{1,0:T(8,128)(2,1)S(1)}, u32[]{:S(2)}, u32[]{:S(2)}) collective-permute-start(bf16[416,512]{1,0:T(8,128)(2,1)} %get-tuple-element.104), channel_id=1, source_target_pairs={{0,2},{2,4},{4,6},{6,8},{8,10},{10,12},{12,14},{14,0},{1,3},{3,5},... | collective-permute-start | bytes 1277960 | tf_op jit(solution)/shard_map/ppermute | solution.py:920
  287.0 16.7 %collective-permute-start.7 = (bf16[416,512]{1,0:T(8,128)(2,1)}, bf16[416,512]{1,0:T(8,128)(2,1)S(1)}, u32[]{:S(2)}, u32[]{:S(2)}) collective-permute-start(bf16[416,512]{1,0:T(8,128)(2,1)} %get-tuple-element.105), channel_id=1, source_target_pairs={{0,4},{2,6},{4,8},{6,10},{8,12},{10,14},{12,0},{14,2},{1,5},{3,7},... | collective-permute-start | bytes 1277960 | tf_op jit(solution)/shard_map/ppermute | solution.py:920
  287.6 72.4 %collective-permute-start.8 = (bf16[416,512]{1,0:T(8,128)(2,1)}, bf16[416,512]{1,0:T(8,128)(2,1)S(1)}, u32[]{:S(2)}, u32[]{:S(2)}) collective-permute-start(bf16[416,512]{1,0:T(8,128)(2,1)} %get-tuple-element.106), channel_id=1, source_target_pairs={{0,6},{2,8},{4,10},{6,12},{8,14},{10,0},{12,2},{14,4},{1,7},{3,9},... | collective-permute-start | bytes 1277960 | tf_op jit(solution)/shard_map/ppermute | solution.py:920
  301.5 68.4 %copy-start.7 = (bf16[416,512]{1,0:T(8,128)(2,1)}, bf16[416,512]{1,0:T(8,128)(2,1)S(1)}, u32[]{:S(2)}) copy-start(bf16[416,512]{1,0:T(8,128)(2,1)S(1)} %collective-permute-done.6.refs_1_) | copy-start | bytes 1277956
  301.5 80.6 %collective-permute-start.9 = (bf16[416,512]{1,0:T(8,128)(2,1)}, bf16[416,512]{1,0:T(8,128)(2,1)}, u32[]{:S(2)}, u32[]{:S(2)}) collective-permute-start(bf16[416,512]{1,0:T(8,128)(2,1)} %get-tuple-element.107), channel_id=1, source_target_pairs={{0,8},{2,10},{4,12},{6,14},{8,0},{10,2},{12,4},{14,6},{1,9},{3,11}... | collective-permute-start | bytes 1277960 | tf_op jit(solution)/shard_map/ppermute | solution.py:920
  303.6 66.3 %copy-start.8 = (bf16[416,512]{1,0:T(8,128)(2,1)}, bf16[416,512]{1,0:T(8,128)(2,1)S(1)}, u32[]{:S(2)}) copy-start(bf16[416,512]{1,0:T(8,128)(2,1)S(1)} %collective-permute-done.7.refs_2_) | copy-start | bytes 1277956
  303.6 78.5 %collective-permute-start.10 = (bf16[416,512]{1,0:T(8,128)(2,1)}, bf16[416,512]{1,0:T(8,128)(2,1)}, u32[]{:S(2)}, u32[]{:S(2)}) collective-permute-start(bf16[416,512]{1,0:T(8,128)(2,1)} %get-tuple-element.108), channel_id=1, source_target_pairs={{0,10},{2,12},{4,14},{6,0},{8,2},{10,4},{12,6},{14,8},{1,11},{3,13... | collective-permute-start | bytes 1277960 | tf_op jit(solution)/shard_map/ppermute | solution.py:920
  360.0 10.0 %copy-start.9 = (bf16[416,512]{1,0:T(8,128)(2,1)}, bf16[416,512]{1,0:T(8,128)(2,1)S(1)}, u32[]{:S(2)}) copy-start(bf16[416,512]{1,0:T(8,128)(2,1)S(1)} %collective-permute-done.8.refs_3_) | copy-start | bytes 1277956
  360.0 22.2 %collective-permute-start.11 = (bf16[416,512]{1,0:T(8,128)(2,1)}, bf16[416,512]{1,0:T(8,128)(2,1)}, u32[]{:S(2)}, u32[]{:S(2)}) collective-permute-start(bf16[416,512]{1,0:T(8,128)(2,1)} %get-tuple-element.109), channel_id=1, source_target_pairs={{0,12},{2,14},{4,0},{6,2},{8,4},{10,6},{12,8},{14,10},{1,13},{3,15... | collective-permute-start | bytes 1277960 | tf_op jit(solution)/shard_map/ppermute | solution.py:920
  370.0 1.2 copy-start.5
  371.2 16.0 %collective-permute-start.12 = (bf16[416,512]{1,0:T(8,128)(2,1)}, bf16[416,512]{1,0:T(8,128)(2,1)}, u32[]{:S(2)}, u32[]{:S(2)}) collective-permute-start(bf16[416,512]{1,0:T(8,128)(2,1)} %get-tuple-element.110), channel_id=1, source_target_pairs={{0,14},{2,0},{4,2},{6,4},{8,6},{10,8},{12,10},{14,12},{1,15},{3,1}... | collective-permute-start | bytes 1277960 | tf_op jit(solution)/shard_map/ppermute | solution.py:920
  382.0 8.4 %copy-start.2 = (bf16[8,208,512]{2,1,0:T(8,128)(2,1)S(1)}, bf16[8,208,512]{2,1,0:T(8,128)(2,1)}, u32[]{:S(2)}) copy-start(bf16[8,208,512]{2,1,0:T(8,128)(2,1)} %get-tuple-element.127.refs_0_.refs_4_.refs_8_.refs_12_) | copy-start | bytes 5111812
  382.0 12.2 %copy-start.4 = (bf16[8,208,512]{2,1,0:T(8,128)(2,1)}, bf16[8,208,512]{2,1,0:T(8,128)(2,1)S(1)}, u32[]{:S(2)}) copy-start(bf16[8,208,512]{2,1,0:T(8,128)(2,1)S(1)} %collective-permute-done.16.refs_1_.refs_5_.refs_9_.refs_13_) | copy-start | bytes 5111812
  382.1 10.1 %collective-permute-start.18 = (bf16[8,208,512]{2,1,0:T(8,128)(2,1)S(1)}, bf16[8,208,512]{2,1,0:T(8,128)(2,1)}, u32[]{:S(2)}, u32[]{:S(2)}) collective-permute-start(bf16[8,208,512]{2,1,0:T(8,128)(2,1)S(1)} %collective-permute-done.16.refs_1_.refs_5_.refs_9_.refs_13_), channel_id=1, source_target_pairs={{0,1},{1,0},{2,3},{3,2},{4,5},{5,4},{6,7},{7,6},{8,9},{9,8},{10,11... | collective-permute-start | bytes 5111816 | tf_op jit(solution)/shard_map/ppermute | solution.py:998
  390.4 3.8 collective-permute-start.17
  390.5 12.5 %collective-permute-start.15 = (bf16[416,512]{1,0:T(8,128)(2,1)}, bf16[416,512]{1,0:T(8,128)(2,1)}, u32[]{:S(2)}, u32[]{:S(2)}) collective-permute-start(bf16[416,512]{1,0:T(8,128)(2,1)} %get-tuple-element.124), channel_id=1, source_target_pairs={{0,16},{16,0},{1,17},{17,1},{2,18},{18,2},{3,19},{19,3},{4,20},{20... | collective-permute-start | bytes 1277960 | tf_op jit(solution)/shard_map/ppermute | solution.py:1027
  394.2 11.1 %copy-start.1 = (bf16[1,128]{1,0:T(2,128)(2,1)S(1)}, bf16[1,128]{1,0:T(2,128)(2,1)}, u32[]{:S(2)}) copy-start(bf16[1,128]{1,0:T(2,128)(2,1)} %param.27) | copy-start | bytes 772
Sparse Core Ops, SparseCore 0:
  11.5 101.1 all-gather.2
  223.7 120.2 reduce-scatter.1
